TPU v7x, 512 devices: a whole 4x4x16 slice. The times are simulated.
512 devices in a mesh: ang: 8 (over x, z_hi), slab: 64 (over y, z_lo, core).
Axes of the slice: x: 4, y: 4, z: 16 (z_hi: 2, z_lo: 8; z = z_hi * 8 + z_lo), core: 2. Of those that a mesh axis runs over, the one named last changes fastest.
Arguments:
- weights: float32 [16, 4, 256], P('ang', None, 'slab'), may hold values from 0.05 to 1
- shifts: int32 [8, 64], P('ang', 'slab'), may hold values from 0 to 1, as said below
- bands: int32 [8, 64], P('ang', 'slab'), may hold values from 1 to 4, as said below
- volume: float32 [256, 64, 1024], P('slab'), may hold values from -6 to 6
- measured: bfloat16 [16, 128, 64, 1024], P('ang', 'slab'), may hold values from -12 to 12
Outputs:
- updated: float32 [256, 64, 1024], P('slab')
- residual: float32 [16, 128, 64, 1024], P('ang', 'slab')
Inputs may be any that keep to these rules, and one draw needn't show every extreme that they name: `shifts`: each band starts within the first 2 rows counted from its slab's first row. shifts plus bands never exceeds 2 * 2, so each band lies in the detector rows of its slab and of the next slab.
All inputs are finite; a program needn't handle non-finite values.
Results may differ from a plain program's by a relative error of at most 0.0003.
Values sent between devices are 32-bit elements; how exact they have to be, the bound alone decides.
No kernel may reach another device: no remote copies, remote signals or barrier semaphores. Data moves between devices by JAX's collectives and lax.ppermute only.
A program may use at most 64 MiB of HBM per device.

v0:
```python
import jax
import jax.numpy as jnp
from jax import lax
from jax.experimental import pallas as pl
from jax.experimental.pallas import tpu as pltpu
from jax.sharding import PartitionSpec as P

TILE = 8
LANES = 128
HALO = 2


def from_behind(block, axis, distance):
    devices = range(lax.axis_size(axis))
    route = [(i - distance, i) for i in devices if i - distance in devices]
    return lax.ppermute(block, axis, route)


def ring_groups():
    count = lax.axis_size("ang")
    return [list(range(0, count, 2)), list(range(1, count, 2))]


def over_ring(pieces):
    return lax.all_to_all(
        pieces, "ang", split_axis=0, concat_axis=0, axis_index_groups=ring_groups()
    )


ROW = 16


def route(pairs):
    count, slabs = lax.axis_size("ang"), lax.axis_size("slab")
    return [
        (a * slabs + s, (a if s // ROW == t // ROW else a ^ 1) * slabs + t)
        for a in range(count)
        for s, t in pairs
        if 0 <= t < slabs
    ]


def from_far(block):
    return lax.ppermute(block, "ang", [(a, a ^ 1) for a in range(lax.axis_size("ang"))])


def to_next(block):
    pairs = [(s, s + 1) for s in range(lax.axis_size("slab"))]
    return lax.ppermute(block, ("ang", "slab"), route(pairs))


def over_ring(pieces):
    return lax.all_to_all(
        pieces, "ang", split_axis=0, concat_axis=0, axis_index_groups=ring_groups()
    )


ROW = 16


def route(pairs):
    count, slabs = lax.axis_size("ang"), lax.axis_size("slab")
    return [
        (a * slabs + s, (a if s // ROW == t // ROW else a ^ 1) * slabs + t)
        for a in range(count)
        for s, t in pairs
        if 0 <= t < slabs
    ]


def from_far(block):
    return lax.ppermute(block, "ang", [(a, a ^ 1) for a in range(lax.axis_size("ang"))])


def within_chip(block):
    return lax.ppermute(block, "slab", [(s, s ^ 1) for s in range(lax.axis_size("slab"))])


def across_chips(block):
    pairs = [(s, s + 1 if s % 2 else s - 1) for s in range(lax.axis_size("slab"))]
    return lax.ppermute(block, ("ang", "slab"), route(pairs))


def to_next(block):
    pairs = [(s, s + 1) for s in range(lax.axis_size("slab"))]
    return lax.ppermute(block, ("ang", "slab"), route(pairs))


def to_previous(block):
    pairs = [(s, s - 1) for s in range(lax.axis_size("slab"))]
    return lax.ppermute(block, ("ang", "slab"), route(pairs))


VMEM = pl.BlockSpec(memory_space=pltpu.VMEM)
SMEM = pl.BlockSpec(memory_space=pltpu.SMEM)
ANY = pl.BlockSpec(memory_space=pl.ANY)


def splats(ref):
    rows, columns = ref.shape
    return [[jnp.full((TILE, LANES), ref[k, z]) for z in range(columns)] for k in range(rows)]


def combine(planes, coefs):
    total = planes[0] * coefs[0]
    for plane, coef in zip(planes[1:], coefs[1:]):
        total = total + plane * coef
    return total


def pack_kernel(coef_ref, window_ref, volume_ref, measured_ref, out_ref):
    angles, rows, height, columns = measured_ref.shape
    layers = volume_ref.shape[0]
    depth = 2 * TILE
    coefs = splats(coef_ref)
    out_ref[angles * rows * height :, :] = window_ref[...]

    def chunk(i, carry):
        top = pl.multiple_of(i * depth, depth)
        for t in range(columns // LANES):
            lanes = pl.ds(t * LANES, LANES)
            planes = [volume_ref[z, pl.ds(top, depth), lanes] for z in range(layers)]
            for a in range(angles):
                for r in range(rows):
                    k = a * rows + r
                    value = measured_ref[a, r, pl.ds(top, depth), lanes].astype(jnp.float32)
                    for j in range(depth // TILE):
                        tile = slice(j * TILE, (j + 1) * TILE)
                        row = pl.multiple_of(k * height + top + j * TILE, TILE)
                        out_ref[pl.ds(row, TILE), lanes] = value[tile] - combine(
                            [plane[tile] for plane in planes], coefs[k]
                        )
        return carry

    lax.fori_loop(0, height // depth, chunk, 0)


def pack(coefs, window, volume, measured):
    angles, rows, height, columns = measured.shape
    return pl.pallas_call(
        pack_kernel,
        in_specs=[SMEM, VMEM, VMEM, VMEM],
        out_specs=VMEM,
        out_shape=jax.ShapeDtypeStruct((angles * rows * height + TILE, columns), jnp.float32),
        compiler_params=pltpu.CompilerParams(vmem_limit_bytes=8 * 2**20),
        name="pack",
    )(coefs, window, volume, measured)


def spread_kernel(coef_ref, sums_ref, own_ref, next_ref, earlier_ref, out_ref):
    count, layers = coef_ref.shape
    ring = out_ref.shape[0]
    columns = own_ref.shape[1]
    height = (own_ref.shape[0] - TILE) // (count // 2)
    depth = height // ring
    ytiles, xtiles = depth // TILE, columns // LANES
    coefs = splats(coef_ref)
    body = layers * ytiles * xtiles * TILE

    def chunk(i, carry):
        top = i * depth
        for t in range(xtiles):
            lanes = pl.ds(t * LANES, LANES)
            for j in range(ytiles):
                planes = [
                    ref[pl.ds(pl.multiple_of(k * height + top + j * TILE, TILE), TILE), lanes]
                    for ref in (own_ref, next_ref)
                    for k in range(count // 2)
                ]
                for z in range(layers):
                    row = ((z * ytiles + j) * xtiles + t) * TILE
                    out_ref[i, row : row + TILE, :] = combine(planes, [c[z] for c in coefs])
        out_ref[i, body : body + TILE, :] = sums_ref[...]
        return carry

    lax.fori_loop(0, ring, chunk, 0)


def spread(coefs, sums, own, following, earlier, height, ring):
    layers, columns = coefs.shape[1], own.shape[1]
    length = layers * (height // ring) * columns // LANES + TILE
    return pl.pallas_call(
        spread_kernel,
        in_specs=[SMEM, VMEM, VMEM, VMEM, ANY],
        out_specs=VMEM,
        out_shape=jax.ShapeDtypeStruct((ring, length, LANES), jnp.float32),
        compiler_params=pltpu.CompilerParams(vmem_limit_bytes=8 * 2**20),
        name="spread",
    )(coefs, sums, own, following, earlier)


def gather_kernel(parts_ref, mine_ref):
    ring, length, _ = parts_ref.shape
    step = next(n for n in (5 * TILE, 3 * TILE, TILE) if length % n == 0)

    def add(i, carry):
        rows = pl.ds(pl.multiple_of(i * step, TILE), step)
        total = parts_ref[0, rows, :]
        for part in range(1, ring):
            total = total + parts_ref[part, rows, :]
        mine_ref[rows, :] = total
        return carry

    lax.fori_loop(0, length // step, add, 0)


def gather(parts):
    return pl.pallas_call(
        gather_kernel,
        in_specs=[VMEM],
        out_specs=VMEM,
        out_shape=jax.ShapeDtypeStruct(parts.shape[1:], jnp.float32),
        compiler_params=pltpu.CompilerParams(vmem_limit_bytes=8 * 2**20),
        name="gather",
    )(parts)


def piece_kernel(place_ref, volume_ref, earlier_ref, out_ref):
    layers, depth, _ = out_ref.shape
    top = pl.multiple_of(place_ref[0] * depth, depth)
    for z in range(layers):
        out_ref[z] = volume_ref[z, pl.ds(top, depth), :]


def piece_of(place, volume, earlier, depth):
    layers, _, columns = volume.shape
    return pl.pallas_call(
        piece_kernel,
        in_specs=[SMEM, VMEM, ANY],
        out_specs=VMEM,
        out_shape=jax.ShapeDtypeStruct((layers, depth, columns), jnp.float32),
        compiler_params=pltpu.CompilerParams(vmem_limit_bytes=8 * 2**20),
        cost_estimate=pl.CostEstimate(flops=0, bytes_accessed=32 * 2**20, transcendentals=0),
        name="piece",
    )(place, volume, earlier)


def late_kernel(volume_ref, earlier_ref, whole_ref):
    for z in range(volume_ref.shape[0]):
        whole_ref[z] = volume_ref[z]


def late(volume, earlier):
    return pl.pallas_call(
        late_kernel,
        in_specs=[VMEM, ANY],
        out_specs=VMEM,
        out_shape=jax.ShapeDtypeStruct(volume.shape, jnp.float32),
        compiler_params=pltpu.CompilerParams(vmem_limit_bytes=8 * 2**20),
        cost_estimate=pl.CostEstimate(flops=0, bytes_accessed=32 * 2**20, transcendentals=0),
        name="late",
    )(volume, earlier)


def residual_kernel(coef_ref, before_ref, own_ref, out_ref, done_ref):
    done_ref[...] = jnp.zeros_like(done_ref)
    angles, rows, height, columns = out_ref.shape
    layers = before_ref.shape[0]
    depth = 2 * TILE
    coefs = [[coef_ref[k, z] for z in range(layers)] for k in range(angles * rows)]

    def chunk(i, carry):
        top = pl.multiple_of(i * depth, depth)
        for t in range(columns // LANES):
            lanes = pl.ds(t * LANES, LANES)
            planes = [before_ref[z, pl.ds(top, depth), lanes] for z in range(layers)]
            for a in range(angles):
                for r in range(rows):
                    k = a * rows + r
                    total = planes[0] * coefs[k][0]
                    for z in range(1, layers):
                        total = total + planes[z] * coefs[k][z]
                    row = pl.multiple_of(k * height + top, depth)
                    out_ref[a, r, pl.ds(top, depth), lanes] = (
                        own_ref[pl.ds(row, depth), lanes] - total
                    )
        return carry

    lax.fori_loop(0, height // depth, chunk, 0)


def residual_of(coefs, before, own, shape):
    return pl.pallas_call(
        residual_kernel,
        in_specs=[SMEM, VMEM, VMEM],
        out_specs=[VMEM, VMEM],
        out_shape=[
            jax.ShapeDtypeStruct(shape, jnp.float32),
            jax.ShapeDtypeStruct((TILE, LANES), jnp.float32),
        ],
        compiler_params=pltpu.CompilerParams(vmem_limit_bytes=8 * 2**20),
        cost_estimate=pl.CostEstimate(flops=0, bytes_accessed=16 * 2**20, transcendentals=0),
        name="residual",
    )(coefs, before, own)


def update_kernel(near_ref, far_ref, before_ref, piece_ref, out_ref):
    copies, layers, depth, columns = out_ref.shape
    ytiles, xtiles = depth // TILE, columns // LANES
    body = layers * ytiles * xtiles * TILE
    sums = near_ref[body:, :] + far_ref[body:, :]
    share = 1.0 / sums[:, 2 * layers : 2 * layers + 1]
    sums = sums * share

    def splat(value):
        return jnp.broadcast_to(value, (TILE, LANES))

    shares = [splat(share[z : z + 1, :]) for z in range(layers)]
    coefs = [
        [splat(sums[z : z + 1, k : k + 1]) for k in range(2 * layers)] for z in range(layers)
    ]
    for t in range(xtiles):
        lanes = pl.ds(t * LANES, LANES)
        for j in range(ytiles):
            rows = pl.ds(j * TILE, TILE)
            planes = [ref[z, rows, lanes] for ref in (before_ref, piece_ref) for z in range(layers)]
            for z in range(layers):
                row = ((z * ytiles + j) * xtiles + t) * TILE
                total = (near_ref[row : row + TILE, :] + far_ref[row : row + TILE, :]) * shares[z]
                value = planes[layers + z] + (total - combine(planes, coefs[z]))
                for copy in range(copies):
                    out_ref[copy, z, rows, lanes] = value


def update(near, far, before, piece, ring):
    return pl.pallas_call(
        update_kernel,
        in_specs=[VMEM] * 4,
        out_specs=VMEM,
        out_shape=jax.ShapeDtypeStruct((ring,) + piece.shape, jnp.float32),
        compiler_params=pltpu.CompilerParams(vmem_limit_bytes=8 * 2**20),
        name="update",
    )(near, far, before, piece)


def sweep(source, target, edge, lowest, highest):
    tall, columns = source.shape[1:]
    height = tall - TILE
    xtiles = columns // LANES
    lane = lax.broadcasted_iota(jnp.int32, (TILE, LANES), 1)
    level = lax.broadcasted_iota(jnp.int32, (TILE, LANES), 0)
    last_lane, first_lane = lane == LANES - 1, lane == 0
    last_row, first_row = level == TILE - 1, level == 0
    spans = [pl.ds(t * LANES, LANES) for t in range(xtiles)]
    for z in range(lowest, highest + 1):
        edge[z, :, :] = jnp.zeros((TILE, columns), jnp.float32)

    def band(i, carry):
        top = pl.multiple_of(i * TILE, TILE)
        rows = pl.ds(top, TILE)
        below = pl.ds(top + TILE, 1)
        upper = [source[lowest - 1, rows, span] for span in spans]
        flow_z = None
        for z in range(lowest - 1, highest + 1):
            base, upper = upper, [source[z + 1, rows, span] for span in spans]
            turned = [pltpu.roll(b, LANES - 1, 1) for b in base]
            grad_z, along, scaled = [], [], []
            for t in range(xtiles):
                rise = upper[t] - base[t]
                nearby = jnp.where(
                    last_row,
                    jnp.broadcast_to(source[z, below, spans[t]], (TILE, LANES)),
                    pltpu.roll(base[t], TILE - 1, 0),
                )
                down = nearby - base[t]
                right = jnp.where(
                    last_lane, turned[t + 1] if t + 1 < xtiles else base[t], turned[t]
                )
                across = right - base[t]
                scale = lax.rsqrt(rise * rise + down * down + across * across + 0.01)
                grad_z.append(rise * scale)
                along.append(down * scale)
                scaled.append(across * scale)
            if z >= lowest:
                moved = [pltpu.roll(p, 1, 1) for p in scaled]
                for t in range(xtiles):
                    left = jnp.where(first_lane, moved[t - 1] if t else 0.0, moved[t])
                    above = jnp.where(
                        first_row,
                        jnp.broadcast_to(edge[z, TILE - 1 : TILE, spans[t]], (TILE, LANES)),
                        pltpu.roll(along[t], 1, 0),
                    )
                    edge[z, :, spans[t]] = along[t]
                    div = (grad_z[t] - flow_z[t]) + (along[t] - above) + (scaled[t] - left)
                    target(z, rows, spans[t], base[t] + 0.05 * div)
            flow_z = grad_z
        return carry

    lax.fori_loop(0, height // TILE, band, 0)


def smooth_kernel(place_ref, earlier_ref, own_ref, low_ref, high_ref, out_ref, field, middle, edge):
    ring, layers, depth, columns = own_ref.shape
    height = ring * depth
    keep_low = place_ref[1].astype(jnp.float32)
    keep_high = place_ref[2].astype(jnp.float32)

    def fill(i, carry):
        top = pl.multiple_of(i * depth, depth)
        for z in range(HALO):
            field[z, pl.ds(top, depth), :] = low_ref[i, z]
            field[HALO + layers + z, pl.ds(top, depth), :] = high_ref[i, z]
        for z in range(layers):
            field[HALO + z, pl.ds(top, depth), :] = own_ref[i, z]
        return carry

    lax.fori_loop(0, ring, fill, 0)
    for z in range(layers + 2 * HALO):
        field[z, height : height + 1, :] = field[z, height - 1 : height, :]

    def keep(z, rows, span, value):
        if z == HALO - 1:
            value = value * keep_low
        if z == HALO + layers:
            value = value * keep_high
        middle[z, rows, span] = value

    def finish(z, rows, span, value):
        out_ref[z - HALO, rows, span] = value

    sweep(field, keep, edge, HALO - 1, HALO + layers)
    for z in range(HALO - 1, HALO + layers + 1):
        middle[z, height : height + 1, :] = middle[z, height - 1 : height, :]
    sweep(middle, finish, edge, HALO, HALO + layers - 1)


def smooth(place, earlier, own, low, high):
    ring, layers, depth, columns = own.shape
    deep, height = layers + 2 * HALO, ring * depth
    return pl.pallas_call(
        smooth_kernel,
        in_specs=[SMEM, ANY, VMEM, VMEM, VMEM],
        out_specs=VMEM,
        out_shape=jax.ShapeDtypeStruct((layers, height, columns), jnp.float32),
        scratch_shapes=[
            pltpu.VMEM((deep, height + TILE, columns), jnp.float32),
            pltpu.VMEM((deep, height + TILE, columns), jnp.float32),
            pltpu.VMEM((deep, TILE, columns), jnp.float32),
        ],
        compiler_params=pltpu.CompilerParams(vmem_limit_bytes=16 * 2**20),
        name="smooth",
    )(place, earlier, own, low, high)


def windows(weights, shifts, bands):
    band_rows = weights.shape[1]
    rows_i = jnp.arange(band_rows, dtype=jnp.int32)[:, None]
    rows_j = jnp.arange(band_rows, dtype=jnp.int32)[None, :]
    placer = ((rows_i == rows_j + shifts[0, 0]) & (rows_j < bands[0, 0])).astype(jnp.float32)
    return jnp.sum(placer[None, :, :, None] * weights[:, None, :, :], axis=2)


def per_device(weights, shifts, bands, volume, measured):
    layers, height, columns = volume.shape
    own_rows = measured.shape[1]
    ring = lax.axis_size("ang") // 2
    depth = height // ring
    slab = lax.axis_index("slab")
    last_slab = lax.axis_size("slab") - 1
    place = jnp.stack(
        [lax.axis_index("ang") // 2, slab > 0, slab < last_slab]
    ).astype(jnp.int32)

    window = windows(weights, shifts, bands)
    low, high = window[:, :own_rows], window[:, own_rows:]
    count = window.shape[0] * own_rows
    flat = lambda block: block.reshape(count, layers)
    line = jnp.pad(window.reshape(1, -1), ((0, TILE - 1), (0, columns - window.size)))
    back = pack(flat(low), line, volume, measured)
    following = from_behind(back, "slab", -1)
    window_before = from_behind(window, "slab", 1)
    piece = piece_of(place, volume, back, depth)
    before = to_next(piece)
    window_after = following[-TILE, : window.size].reshape(window.shape)

    low_after, high_before = window_after[:, :own_rows], window_before[:, own_rows:]
    total_own = jnp.sum(low, axis=2) + jnp.sum(high_before, axis=2)
    total_next = jnp.sum(low_after, axis=2) + jnp.sum(high, axis=2)
    share_own = 1.0 / jnp.maximum(total_own, 1.0)
    share_next = jnp.where(slab < last_slab, 1.0 / jnp.maximum(total_next, 1.0), 0.0)
    coefs_own = flat(low) * share_own.reshape(count, 1)
    coefs_next = flat(high) * share_next.reshape(count, 1)
    back_coefs = jnp.concatenate([coefs_own, coefs_next])
    normal_before = jnp.sum(coefs_own[:, :, None] * flat(high_before)[:, None, :], axis=0)
    normal_own = jnp.sum(coefs_next[:, :, None] * flat(high)[:, None, :], axis=0)
    column_part = jnp.sum(window, axis=(0, 1))
    sums = jnp.concatenate([normal_before, normal_own, column_part[:, None]], axis=1)
    sums = jnp.pad(sums, ((0, TILE - layers), (0, LANES - 2 * layers - 1)))

    sent = spread(back_coefs, sums, back, following, before, height, ring)
    near = gather(over_ring(sent))
    pieces = update(near, from_far(near), before, piece, ring)
    field = over_ring(pieces)
    volume_before = to_next(late(volume, pieces))
    residual, done = residual_of(flat(high_before), volume_before, back, measured.shape)
    halo_low = to_next(field[:, layers - HALO :])
    halo_high = to_previous(field[:, :HALO])
    updated = smooth(place, done, field, halo_low, halo_high)
    return (updated, residual)


def solution(mesh):
    return jax.shard_map(
        per_device,
        mesh=mesh,
        in_specs=(
            P("ang", None, "slab"),
            P("ang", "slab"),
            P("ang", "slab"),
            P("slab", None, None),
            P("ang", "slab", None, None),
        ),
        out_specs=(P("slab", None, None), P("ang", "slab", None, None)),
        check_vma=False,
    )
```

profile of v0, /device:TPU:145, one launch (start us, length us, event | category | flops | bytes accessed | tf_op | source)
XLA Modules:
  0.0 124.7 jit_solution(1275080645180429162)
XLA Ops:
  2.0 0.8 multiply_reduce_fusion
  2.7 0.1 slice_reduce_fusion.3
  2.9 1.2 copy-done
  4.2 1.0 copy-done.2
  5.2 0.9 pack.1.earlier_ref.own_ref
  6.1 2.6 %collective-permute-start.1 = (f32[264,1024]{1,0:T(8,128)S(1)}, f32[264,1024]{1,0:T(8,128)S(1)}, u32[]{:S(2)}, u32[]{:S(2)}) collective-permute-start(f32[264,1024]{1,0:T(8,128)S(1)} %pack.1.earlier_ref.own_ref), channel_id=1, source_target_pairs={{1,0},{2,1},{3,2},{4,3},{5,4},{6,5},{7,6},{8,7},{9,8},{10,9},{11,1... | collective-permute-start | bytes 3244040 | tf_op jit(solution)/shard_map/ppermute | solution.py:16
  8.7 3.4 %collective-permute-start = (f32[2,4,4]{2,1,0:T(4,128)S(1)}, f32[2,4,4]{2,1,0:T(4,128)S(1)}, u32[]{:S(2)}, u32[]{:S(2)}) collective-permute-start(f32[2,4,4]{2,1,0:T(4,128)S(1)} %get-tuple-element.7), channel_id=1, source_target_pairs={{0,1},{1,2},{2,3},{3,4},{4,5},{5,6},{6,7},{7,8},{8,9},{9,10},{10,1... | collective-permute-start | bytes 392 | tf_op jit(solution)/shard_map/ppermute | solution.py:16
  12.2 0.6 piece.1.piece_ref
  12.8 2.4 %collective-permute-start.2 = (f32[4,16,1024]{2,1,0:T(8,128)S(1)}, f32[4,16,1024]{2,1,0:T(8,128)}, u32[]{:S(2)}, u32[]{:S(2)}) collective-permute-start(f32[4,16,1024]{2,1,0:T(8,128)S(1)} %piece.1.piece_ref), channel_id=1, source_target_pairs={{0,1},{1,2},{2,3},{3,4},{4,5},{5,6},{6,7},{7,8},{8,9},{9,10},{10,1... | collective-permute-start | bytes 786440 | tf_op jit(solution)/shard_map/ppermute | solution.py:86
  15.2 0.1 copy.8
  15.3 0.1 slice_reduce_fusion.4
  15.6 0.1 multiply_reduce_fusion.3
  15.7 7.8 %collective-permute-done.1.next_ref = f32[264,1024]{1,0:T(8,128)S(1)} collective-permute-done((f32[264,1024]{1,0:T(8,128)S(1)}, f32[264,1024]{1,0:T(8,128)S(1)}, u32[]{:S(2)}, u32[]{:S(2)}) %collective-permute-start.1) | collective-permute-done | bytes 1081376 | tf_op jit(solution)/shard_map/ppermute | solution.py:16
  23.5 0.1 reshape_squeeze.3
  23.6 0.1 slice_reduce_fusion
  23.8 0.1 multiply_reduce_fusion.2
  24.0 6.1 %collective-permute-done.2.earlier_ref.before_ref = f32[4,16,1024]{2,1,0:T(8,128)} collective-permute-done((f32[4,16,1024]{2,1,0:T(8,128)S(1)}, f32[4,16,1024]{2,1,0:T(8,128)}, u32[]{:S(2)}, u32[]{:S(2)}) %collective-permute-start.2) | collective-permute-done | bytes 262176 | tf_op jit(solution)/shard_map/ppermute | solution.py:86
  30.1 1.2 spread.1
  31.3 16.6 %all_to_all.10.parts_ref = f32[4,520,128]{2,1,0:T(8,128)S(1)} all-to-all(f32[4,520,128]{2,1,0:T(8,128)S(1)} %spread.1), channel_id=1, replica_groups={{0,128,256,384},{64,192,320,448},{1,129,257,385},{65,193,321,449},{2,13..., dimensions={0} | all-to-all | bytes 2129920 | tf_op jit(solution)/shard_map/all_to_all | solution.py:53
  47.8 0.1 gather.1.near_ref
  48.0 1.9 %collective-permute-start.3 = (f32[520,128]{1,0:T(8,128)S(1)}, f32[520,128]{1,0:T(8,128)S(1)}, u32[]{:S(2)}, u32[]{:S(2)}) collective-permute-start(f32[520,128]{1,0:T(8,128)S(1)} %gather.1.near_ref), channel_id=1, source_target_pairs={{0,64},{64,0},{128,192},{192,128},{256,320},{320,256},{384,448},{4... | collective-permute-start | bytes 798728 | tf_op jit(solution)/shard_map/ppermute | solution.py:72
  49.9 19.2 %collective-permute-done.3.far_ref = f32[520,128]{1,0:T(8,128)S(1)} collective-permute-done((f32[520,128]{1,0:T(8,128)S(1)}, f32[520,128]{1,0:T(8,128)S(1)}, u32[]{:S(2)}, u32[]{:S(2)}) %collective-permute-start.3) | collective-permute-done | bytes 266272 | tf_op jit(solution)/shard_map/ppermute | solution.py:72
  69.1 2.3 %update.1.earlier_ref = f32[4,4,16,1024]{3,2,1,0:T(8,128)} custom-call(f32[520,128]{1,0:T(8,128)S(1)} %gather.1.near_ref, f32[520,128]{1,0:T(8,128)S(1)} %collective-permute-done.3.far_ref, f32[4,16,1024]{2,1,0:T(8,128)} %collective-permute-done.2.earlier_ref.before_ref, f32[4,16,1024]{2,1,0:T(8,128)S(1)} %piece.1.piece_ref), custom_call_target="tpu_custom_call" | custom-call | tf_op jit(solution)/shard_map/update/pallas_call | solution.py:326
  71.4 3.5 %all-to-all-start.1 = ((f32[4,4,16,1024]{3,2,1,0:T(8,128)}), f32[4,4,16,1024]{3,2,1,0:T(8,128)S(1)}, u32[]{:S(2)}, u32[]{:S(2)}) async-start(f32[4,4,16,1024]{3,2,1,0:T(8,128)} %update.1.earlier_ref), calls=%async_computation.1 | async-start | bytes 2097152 | tf_op jit(solution)/shard_map/all_to_all | solution.py:53
  74.9 1.0 late.1
  75.9 19.6 %collective-permute-start.4 = (f32[4,64,1024]{2,1,0:T(8,128)}, f32[4,64,1024]{2,1,0:T(8,128)S(1)}, u32[]{:S(2)}, u32[]{:S(2)}) collective-permute-start(f32[4,64,1024]{2,1,0:T(8,128)} %late.1), channel_id=1, source_target_pairs={{0,1},{1,2},{2,3},{3,4},{4,5},{5,6},{6,7},{7,8},{8,9},{9,10},{10,1... | collective-permute-start | bytes 3145736 | tf_op jit(solution)/shard_map/ppermute | solution.py:86
  95.7 13.6 %collective-permute-start.5 = (f32[4,2,16,1024]{3,2,1,0:T(8,128)S(1)}, f32[4,2,16,1024]{3,2,1,0:T(8,128)S(1)}, u32[]{:S(2)}, u32[]{:S(2)}) collective-permute-start(f32[4,2,16,1024]{3,2,1,0:T(8,128)S(1)} %get-tuple-element.11), channel_id=1, source_target_pairs={{0,1},{1,2},{2,3},{3,4},{4,5},{5,6},{6,7},{7,8},{8,9},{9,10},{10,1... | collective-permute-start | bytes 1572872 | tf_op jit(solution)/shard_map/ppermute | solution.py:86
  109.3 1.9 %collective-permute-start.6 = (f32[4,2,16,1024]{3,2,1,0:T(8,128)S(1)}, f32[4,2,16,1024]{3,2,1,0:T(8,128)S(1)}, u32[]{:S(2)}, u32[]{:S(2)}) collective-permute-start(f32[4,2,16,1024]{3,2,1,0:T(8,128)S(1)} %get-tuple-element.10), channel_id=1, source_target_pairs={{1,0},{2,1},{3,2},{4,3},{5,4},{6,5},{7,6},{8,7},{9,8},{10,9},{11,1... | collective-permute-start | bytes 1572872 | tf_op jit(solution)/shard_map/ppermute | solution.py:91
  111.2 1.8 %residual.1 = (f32[2,2,64,1024]{3,2,1,0:T(8,128)}, f32[8,128]{1,0:T(8,128)S(1)}) custom-call(f32[4,4]{1,0:T(4,128)S(1)} %bitcast.14, f32[4,64,1024]{2,1,0:T(8,128)S(1)} %collective-permute-done.4.before_ref, f32[264,1024]{1,0:T(8,128)S(1)} %pack.1.earlier_ref.own_ref), custom_call_target="tpu_custom_call" | custom-call | bytes 16777216 | tf_op jit(solution)/shard_map/residual/pallas_call | solution.py:283
  113.0 2.3 %collective-permute-done.5.low_ref = f32[4,2,16,1024]{3,2,1,0:T(8,128)S(1)} collective-permute-done((f32[4,2,16,1024]{3,2,1,0:T(8,128)S(1)}, f32[4,2,16,1024]{3,2,1,0:T(8,128)S(1)}, u32[]{:S(2)}, u32[]{:S(2)}) %collective-permute-start.5) | collective-permute-done | bytes 524320 | tf_op jit(solution)/shard_map/ppermute | solution.py:86
  115.4 4.4 %collective-permute-done.6.high_ref = f32[4,2,16,1024]{3,2,1,0:T(8,128)S(1)} collective-permute-done((f32[4,2,16,1024]{3,2,1,0:T(8,128)S(1)}, f32[4,2,16,1024]{3,2,1,0:T(8,128)S(1)}, u32[]{:S(2)}, u32[]{:S(2)}) %collective-permute-start.6) | collective-permute-done | bytes 524320 | tf_op jit(solution)/shard_map/ppermute | solution.py:91
  119.8 5.0 %smooth.1 = f32[4,64,1024]{2,1,0:T(8,128)} custom-call(s32[3]{0:T(128)S(1)} %pad_add_fusion.place_ref, f32[8,128]{1,0:T(8,128)S(1)} %get-tuple-element.4.earlier_ref, f32[4,4,16,1024]{3,2,1,0:T(8,128)S(1)} %all-to-all-done.1.own_ref, f32[4,2,16,1024]{3,2,1,0:T(8,128)S(1)} %collective-permute-done.5.low_ref, ...), custom_call_target="tpu_custom_call" | custom-call | tf_op jit(solution)/shard_map/smooth/pallas_call | solution.py:430
  (23 shorter events, 0.7 us)
Async XLA Ops:
  2.9 1.2 copy-start
  4.2 1.0 copy-start.2
  5.2 7.1 %copy-start.1 = (f32[4,64,1024]{2,1,0:T(8,128)S(1)}, f32[4,64,1024]{2,1,0:T(8,128)}, u32[]{:S(2)}) copy-start(f32[4,64,1024]{2,1,0:T(8,128)} %volume_ref.5) | copy-start | bytes 3145732
  6.1 17.3 %collective-permute-start.1 = (f32[264,1024]{1,0:T(8,128)S(1)}, f32[264,1024]{1,0:T(8,128)S(1)}, u32[]{:S(2)}, u32[]{:S(2)}) collective-permute-start(f32[264,1024]{1,0:T(8,128)S(1)} %pack.1.earlier_ref.own_ref), channel_id=1, source_target_pairs={{1,0},{2,1},{3,2},{4,3},{5,4},{6,5},{7,6},{8,7},{9,8},{10,9},{11,1... | collective-permute-start | bytes 3244040 | tf_op jit(solution)/shard_map/ppermute | solution.py:16
  8.7 6.6 %collective-permute-start = (f32[2,4,4]{2,1,0:T(4,128)S(1)}, f32[2,4,4]{2,1,0:T(4,128)S(1)}, u32[]{:S(2)}, u32[]{:S(2)}) collective-permute-start(f32[2,4,4]{2,1,0:T(4,128)S(1)} %get-tuple-element.7), channel_id=1, source_target_pairs={{0,1},{1,2},{2,3},{3,4},{4,5},{5,6},{6,7},{7,8},{8,9},{9,10},{10,1... | collective-permute-start | bytes 392 | tf_op jit(solution)/shard_map/ppermute | solution.py:16
  12.8 17.3 %collective-permute-start.2 = (f32[4,16,1024]{2,1,0:T(8,128)S(1)}, f32[4,16,1024]{2,1,0:T(8,128)}, u32[]{:S(2)}, u32[]{:S(2)}) collective-permute-start(f32[4,16,1024]{2,1,0:T(8,128)S(1)} %piece.1.piece_ref), channel_id=1, source_target_pairs={{0,1},{1,2},{2,3},{3,4},{4,5},{5,6},{6,7},{7,8},{8,9},{9,10},{10,1... | collective-permute-start | bytes 786440 | tf_op jit(solution)/shard_map/ppermute | solution.py:86
  48.0 21.1 %collective-permute-start.3 = (f32[520,128]{1,0:T(8,128)S(1)}, f32[520,128]{1,0:T(8,128)S(1)}, u32[]{:S(2)}, u32[]{:S(2)}) collective-permute-start(f32[520,128]{1,0:T(8,128)S(1)} %gather.1.near_ref), channel_id=1, source_target_pairs={{0,64},{64,0},{128,192},{192,128},{256,320},{320,256},{384,448},{4... | collective-permute-start | bytes 798728 | tf_op jit(solution)/shard_map/ppermute | solution.py:72
  71.4 24.2 %all-to-all-start.1 = ((f32[4,4,16,1024]{3,2,1,0:T(8,128)}), f32[4,4,16,1024]{3,2,1,0:T(8,128)S(1)}, u32[]{:S(2)}, u32[]{:S(2)}) async-start(f32[4,4,16,1024]{3,2,1,0:T(8,128)} %update.1.earlier_ref), calls=%async_computation.1 | async-start | bytes 2097152 | tf_op jit(solution)/shard_map/all_to_all | solution.py:53
  75.9 35.2 %collective-permute-start.4 = (f32[4,64,1024]{2,1,0:T(8,128)}, f32[4,64,1024]{2,1,0:T(8,128)S(1)}, u32[]{:S(2)}, u32[]{:S(2)}) collective-permute-start(f32[4,64,1024]{2,1,0:T(8,128)} %late.1), channel_id=1, source_target_pairs={{0,1},{1,2},{2,3},{3,4},{4,5},{5,6},{6,7},{7,8},{8,9},{9,10},{10,1... | collective-permute-start | bytes 3145736 | tf_op jit(solution)/shard_map/ppermute | solution.py:86
  95.7 19.7 %collective-permute-start.5 = (f32[4,2,16,1024]{3,2,1,0:T(8,128)S(1)}, f32[4,2,16,1024]{3,2,1,0:T(8,128)S(1)}, u32[]{:S(2)}, u32[]{:S(2)}) collective-permute-start(f32[4,2,16,1024]{3,2,1,0:T(8,128)S(1)} %get-tuple-element.11), channel_id=1, source_target_pairs={{0,1},{1,2},{2,3},{3,4},{4,5},{5,6},{6,7},{7,8},{8,9},{9,10},{10,1... | collective-permute-start | bytes 1572872 | tf_op jit(solution)/shard_map/ppermute | solution.py:86
  109.3 10.5 %collective-permute-start.6 = (f32[4,2,16,1024]{3,2,1,0:T(8,128)S(1)}, f32[4,2,16,1024]{3,2,1,0:T(8,128)S(1)}, u32[]{:S(2)}, u32[]{:S(2)}) collective-permute-start(f32[4,2,16,1024]{3,2,1,0:T(8,128)S(1)} %get-tuple-element.10), channel_id=1, source_target_pairs={{1,0},{2,1},{3,2},{4,3},{5,4},{6,5},{7,6},{8,7},{9,8},{10,9},{11,1... | collective-permute-start | bytes 1572872 | tf_op jit(solution)/shard_map/ppermute | solution.py:91
where the time goes:
time: 125 us
  starting transfers between devices  49 us (39%)
  waiting for transfers between devices  39.8 us (32%)
  blocking collectives  16.6 us (13%)
  Pallas kernels  12.9 us (10%)
  local copies, waits for them, and re-layouts  2.8 us (2%)
  between operations  2.11 us (2%)
  other arithmetic  1.57 us (1%)
    ppermute x3, starting transfers between devices, to_next(): return lax.ppermute(block, ('ang', 'slab'), route(pairs))  35.6 us
    ppermute x1, waiting for transfers between devices, from_far(): lax.ppermute(block, 'ang', [(a, a ^ 1) for a in range(lax.axis_size('ang'...  19.2 us
    all_to_all x1, blocking collectives, over_ring(): lax.all_to_all(pieces, 'ang', split_axis=0, concat_axis=0, axis_index_gro...  16.6 us
    ppermute x3, waiting for transfers between devices, to_next(): return lax.ppermute(block, ('ang', 'slab'), route(pairs))  8.46 us
    ppermute x2, waiting for transfers between devices, from_behind(): return lax.ppermute(block, axis, route)  7.77 us
    ppermute x2, starting transfers between devices, from_behind(): return lax.ppermute(block, axis, route)  6.03 us
    pallas_call x1, Pallas kernels, smooth(): pl.pallas_call(smooth_kernel, in_specs=[SMEM, ANY, VMEM, VMEM, VMEM], out...  4.95 us
    ppermute x1, waiting for transfers between devices, to_previous(): return lax.ppermute(block, ('ang', 'slab'), route(pairs))  4.4 us
  transfers between devices with their start and end apart: 8, of which 5 were waited for; matrix products, arithmetic and copies ran while one was open for 1% of the time, Pallas kernels for 3%

commit v1 on v0

--- a/solution.py
+++ b/solution.py
@@ -252,7 +252,7 @@
     )(volume, earlier)
 
 
-def residual_kernel(coef_ref, before_ref, own_ref, out_ref, done_ref):
+def residual_kernel(coef_ref, before_ref, own_ref, earlier_ref, out_ref, done_ref):
     done_ref[...] = jnp.zeros_like(done_ref)
     angles, rows, height, columns = out_ref.shape
     layers = before_ref.shape[0]
@@ -279,10 +279,10 @@
     lax.fori_loop(0, height // depth, chunk, 0)
 
 
-def residual_of(coefs, before, own, shape):
+def residual_of(coefs, before, own, earlier, shape):
     return pl.pallas_call(
         residual_kernel,
-        in_specs=[SMEM, VMEM, VMEM],
+        in_specs=[SMEM, VMEM, VMEM, ANY],
         out_specs=[VMEM, VMEM],
         out_shape=[
             jax.ShapeDtypeStruct(shape, jnp.float32),
@@ -291,7 +291,7 @@
         compiler_params=pltpu.CompilerParams(vmem_limit_bytes=8 * 2**20),
         cost_estimate=pl.CostEstimate(flops=0, bytes_accessed=16 * 2**20, transcendentals=0),
         name="residual",
-    )(coefs, before, own)
+    )(coefs, before, own, earlier)
 
 
 def update_kernel(near_ref, far_ref, before_ref, piece_ref, out_ref):
@@ -488,11 +488,13 @@
     sums = jnp.pad(sums, ((0, TILE - layers), (0, LANES - 2 * layers - 1)))
 
     sent = spread(back_coefs, sums, back, following, before, height, ring)
+    volume_before = to_next(late(volume, sent))
     near = gather(over_ring(sent))
     pieces = update(near, from_far(near), before, piece, ring)
     field = over_ring(pieces)
-    volume_before = to_next(late(volume, pieces))
-    residual, done = residual_of(flat(high_before), volume_before, back, measured.shape)
+    residual, done = residual_of(
+        flat(high_before), volume_before, back, pieces, measured.shape
+    )
     halo_low = to_next(field[:, layers - HALO :])
     halo_high = to_previous(field[:, :HALO])
     updated = smooth(place, done, field, halo_low, halo_high)

time: 125 us -> 130 us (1.040)
  the two profiles are of different devices: /device:TPU:145 before, /device:TPU:1 now
where the time goes in v1:
time: 130 us; the launch traced here: 129 us
  starting transfers between devices  75.3 us (58%)
  blocking collectives  15.6 us (12%)
  waiting for transfers between devices  14.5 us (11%)
  Pallas kernels  12.6 us (10%)
  local copies, waits for them, and re-layouts  7.23 us (6%)
  between operations  2.14 us (2%)
  other arithmetic  1.56 us (1%)
    ppermute x3, starting transfers between devices, to_next(): return lax.ppermute(block, ('ang', 'slab'), route(pairs))  45.4 us
    all_to_all x1, blocking collectives, over_ring(): lax.all_to_all(pieces, 'ang', split_axis=0, concat_axis=0, axis_index_gro...  15.6 us
    ppermute x1, starting transfers between devices, from_far(): lax.ppermute(block, 'ang', [(a, a ^ 1) for a in range(lax.axis_size('ang'...  13 us
    ppermute x2, starting transfers between devices, from_behind(): return lax.ppermute(block, axis, route)  10.7 us
    pallas_call x1, Pallas kernels, smooth(): pl.pallas_call(smooth_kernel, in_specs=[SMEM, ANY, VMEM, VMEM, VMEM], out...  5.65 us
    unnamed x14, local copies, waits for them, and re-layouts  5.46 us
    ppermute x1, waiting for transfers between devices, to_previous(): return lax.ppermute(block, ('ang', 'slab'), route(pairs))  4.4 us
    all_to_all x1, starting transfers between devices, over_ring(): lax.all_to_all(pieces, 'ang', split_axis=0, concat_axis=0, axis_index_gro...  4.24 us
  transfers between devices with their start and end apart: 8, of which 4 were waited for; matrix products, arithmetic and copies ran while one was open for 2% of the time, Pallas kernels for 3%

profile of v1, /device:TPU:1, one launch (start us, length us, event | category | flops | bytes accessed | tf_op | source)
XLA Modules:
  0.0 128.9 jit_solution(3180352934908181301)
XLA Ops:
  2.0 0.8 multiply_reduce_fusion
  2.7 0.1 slice_reduce_fusion.3
  2.9 1.2 copy-done
  4.2 1.0 copy-done.6
  5.2 0.9 pack.1.earlier_ref.own_ref
  6.1 8.8 %collective-permute-start.1 = (f32[264,1024]{1,0:T(8,128)S(1)}, f32[264,1024]{1,0:T(8,128)S(1)}, u32[]{:S(2)}, u32[]{:S(2)}) collective-permute-start(f32[264,1024]{1,0:T(8,128)S(1)} %pack.1.earlier_ref.own_ref), channel_id=1, source_target_pairs={{1,0},{2,1},{3,2},{4,3},{5,4},{6,5},{7,6},{8,7},{9,8},{10,9},{11,1... | collective-permute-start | bytes 3244040 | tf_op jit(solution)/shard_map/ppermute | solution.py:16
  14.9 1.9 %collective-permute-start = (f32[2,4,4]{2,1,0:T(4,128)S(1)}, f32[2,4,4]{2,1,0:T(4,128)S(1)}, u32[]{:S(2)}, u32[]{:S(2)}) collective-permute-start(f32[2,4,4]{2,1,0:T(4,128)S(1)} %get-tuple-element.7), channel_id=1, source_target_pairs={{0,1},{1,2},{2,3},{3,4},{4,5},{5,6},{6,7},{7,8},{8,9},{9,10},{10,1... | collective-permute-start | bytes 392 | tf_op jit(solution)/shard_map/ppermute | solution.py:16
  16.9 0.6 piece.1.piece_ref
  17.5 1.9 %collective-permute-start.2 = (f32[4,16,1024]{2,1,0:T(8,128)S(1)}, f32[4,16,1024]{2,1,0:T(8,128)}, u32[]{:S(2)}, u32[]{:S(2)}) collective-permute-start(f32[4,16,1024]{2,1,0:T(8,128)S(1)} %piece.1.piece_ref), channel_id=1, source_target_pairs={{0,1},{1,2},{2,3},{3,4},{4,5},{5,6},{6,7},{7,8},{8,9},{9,10},{10,1... | collective-permute-start | bytes 786440 | tf_op jit(solution)/shard_map/ppermute | solution.py:86
  19.4 0.1 copy.8
  19.5 0.1 slice_reduce_fusion.4
  19.9 4.0 %collective-permute-done.1.next_ref = f32[264,1024]{1,0:T(8,128)S(1)} collective-permute-done((f32[264,1024]{1,0:T(8,128)S(1)}, f32[264,1024]{1,0:T(8,128)S(1)}, u32[]{:S(2)}, u32[]{:S(2)}) %collective-permute-start.1) | collective-permute-done | bytes 1081376 | tf_op jit(solution)/shard_map/ppermute | solution.py:16
  23.9 1.0 copy-done.4
  25.0 0.1 slice_reduce_fusion
  25.4 1.2 copy-done.5
  26.7 1.2 spread.1.earlier_ref
  27.8 15.6 %all_to_all.10.parts_ref = f32[4,520,128]{2,1,0:T(8,128)S(1)} all-to-all(f32[4,520,128]{2,1,0:T(8,128)S(1)} %spread.1.earlier_ref), channel_id=1, replica_groups={{0,128,256,384},{64,192,320,448},{1,129,257,385},{65,193,321,449},{2,13..., dimensions={0} | all-to-all | bytes 2129920 | tf_op jit(solution)/shard_map/all_to_all | solution.py:53
  43.4 0.1 gather.1.near_ref
  43.5 13.0 %collective-permute-start.4 = (f32[520,128]{1,0:T(8,128)S(1)}, f32[520,128]{1,0:T(8,128)S(1)}, u32[]{:S(2)}, u32[]{:S(2)}) collective-permute-start(f32[520,128]{1,0:T(8,128)S(1)} %gather.1.near_ref), channel_id=1, source_target_pairs={{0,64},{64,0},{128,192},{192,128},{256,320},{320,256},{384,448},{4... | collective-permute-start | bytes 798728 | tf_op jit(solution)/shard_map/ppermute | solution.py:72
  56.6 3.8 %collective-permute-done.4.far_ref = f32[520,128]{1,0:T(8,128)S(1)} collective-permute-done((f32[520,128]{1,0:T(8,128)S(1)}, f32[520,128]{1,0:T(8,128)S(1)}, u32[]{:S(2)}, u32[]{:S(2)}) %collective-permute-start.4) | collective-permute-done | bytes 266272 | tf_op jit(solution)/shard_map/ppermute | solution.py:72
  60.4 1.3 %update.1.earlier_ref = f32[4,4,16,1024]{3,2,1,0:T(8,128)S(1)} custom-call(f32[520,128]{1,0:T(8,128)S(1)} %gather.1.near_ref, f32[520,128]{1,0:T(8,128)S(1)} %collective-permute-done.4.far_ref, f32[4,16,1024]{2,1,0:T(8,128)} %collective-permute-done.2.earlier_ref.before_ref, f32[4,16,1024]{2,1,0:T(8,128)S(1)} %piece.1.piece_ref), custom_call_target="tpu_custom_call" | custom-call | tf_op jit(solution)/shard_map/update/pallas_call | solution.py:326
  61.7 1.0 copy-done.2
  62.7 4.2 %all-to-all-start.1 = ((f32[4,4,16,1024]{3,2,1,0:T(8,128)}), f32[4,4,16,1024]{3,2,1,0:T(8,128)}, u32[]{:S(2)}, u32[]{:S(2)}) async-start(f32[4,4,16,1024]{3,2,1,0:T(8,128)} %copy-done.2), calls=%async_computation.1 | async-start | bytes 2097152 | tf_op jit(solution)/shard_map/all_to_all | solution.py:53
  66.9 1.0 late.1
  68.0 29.3 %collective-permute-start.3 = (f32[4,64,1024]{2,1,0:T(8,128)}, f32[4,64,1024]{2,1,0:T(8,128)S(1)}, u32[]{:S(2)}, u32[]{:S(2)}) collective-permute-start(f32[4,64,1024]{2,1,0:T(8,128)} %late.1), channel_id=1, source_target_pairs={{0,1},{1,2},{2,3},{3,4},{4,5},{5,6},{6,7},{7,8},{8,9},{9,10},{10,1... | collective-permute-start | bytes 3145736 | tf_op jit(solution)/shard_map/ppermute | solution.py:86
  97.3 1.3 %fusion.2 = (f32[4,2,16,1024]{3,2,1,0:T(8,128)S(1)}, f32[4,2,16,1024]{3,2,1,0:T(8,128)S(1)}) fusion(f32[4,4,16,1024]{3,2,1,0:T(8,128)} %all-to-all-done.1.own_ref), kind=kLoop, calls=%fused_computation.24 | loop fusion | bytes 2097152 | tf_op jit(solution)/shard_map/slice | solution.py:499
  98.6 14.2 %collective-permute-start.5 = (f32[4,2,16,1024]{3,2,1,0:T(8,128)S(1)}, f32[4,2,16,1024]{3,2,1,0:T(8,128)S(1)}, u32[]{:S(2)}, u32[]{:S(2)}) collective-permute-start(f32[4,2,16,1024]{3,2,1,0:T(8,128)S(1)} %get-tuple-element.11), channel_id=1, source_target_pairs={{0,1},{1,2},{2,3},{3,4},{4,5},{5,6},{6,7},{7,8},{8,9},{9,10},{10,1... | collective-permute-start | bytes 1572872 | tf_op jit(solution)/shard_map/ppermute | solution.py:86
  112.8 1.9 %collective-permute-start.6 = (f32[4,2,16,1024]{3,2,1,0:T(8,128)S(1)}, f32[4,2,16,1024]{3,2,1,0:T(8,128)S(1)}, u32[]{:S(2)}, u32[]{:S(2)}) collective-permute-start(f32[4,2,16,1024]{3,2,1,0:T(8,128)S(1)} %get-tuple-element.10), channel_id=1, source_target_pairs={{1,0},{2,1},{3,2},{4,3},{5,4},{6,5},{7,6},{8,7},{9,8},{10,9},{11,1... | collective-permute-start | bytes 1572872 | tf_op jit(solution)/shard_map/ppermute | solution.py:91
  114.7 1.8 %residual.1 = (f32[2,2,64,1024]{3,2,1,0:T(8,128)}, f32[8,128]{1,0:T(8,128)S(1)}) custom-call(f32[4,4]{1,0:T(4,128)S(1)} %bitcast.14, f32[4,64,1024]{2,1,0:T(8,128)S(1)} %collective-permute-done.3.before_ref, f32[264,1024]{1,0:T(8,128)S(1)} %pack.1.earlier_ref.own_ref, f32[4,4,16,1024]{3,2,1,0:T(8,128)S(1)} %copy-done.3), custom_call_target="tpu_custom_call" | custom-call | bytes 16777216 | tf_op jit(solution)/shard_map/residual/pallas_call | solution.py:283
  116.6 2.3 %collective-permute-done.5.low_ref = f32[4,2,16,1024]{3,2,1,0:T(8,128)S(1)} collective-permute-done((f32[4,2,16,1024]{3,2,1,0:T(8,128)S(1)}, f32[4,2,16,1024]{3,2,1,0:T(8,128)S(1)}, u32[]{:S(2)}, u32[]{:S(2)}) %collective-permute-start.5) | collective-permute-done | bytes 524320 | tf_op jit(solution)/shard_map/ppermute | solution.py:86
  118.9 4.4 %collective-permute-done.6.high_ref = f32[4,2,16,1024]{3,2,1,0:T(8,128)S(1)} collective-permute-done((f32[4,2,16,1024]{3,2,1,0:T(8,128)S(1)}, f32[4,2,16,1024]{3,2,1,0:T(8,128)S(1)}, u32[]{:S(2)}, u32[]{:S(2)}) %collective-permute-start.6) | collective-permute-done | bytes 524320 | tf_op jit(solution)/shard_map/ppermute | solution.py:91
  123.3 5.6 %smooth.1 = f32[4,64,1024]{2,1,0:T(8,128)} custom-call(s32[3]{0:T(128)S(1)} %pad_add_fusion.place_ref, f32[8,128]{1,0:T(8,128)S(1)} %get-tuple-element.4.earlier_ref, f32[4,4,16,1024]{3,2,1,0:T(8,128)} %all-to-all-done.1.own_ref, f32[4,2,16,1024]{3,2,1,0:T(8,128)S(1)} %collective-permute-done.5.low_ref, f32[4,2,16,1024]{3,2,1,0:T(8,128)S(1)} %collective-permute-done.6.high_ref), custom_call_target="tpu_custom_call" | custom-call | tf_op jit(solution)/shard_map/smooth/pallas_call | solution.py:430
  (31 shorter events, 0.9 us)
Async XLA Ops:
  2.9 1.2 copy-start
  4.2 1.0 copy-start.6
  5.2 11.7 %copy-start.1 = (f32[4,64,1024]{2,1,0:T(8,128)S(1)}, f32[4,64,1024]{2,1,0:T(8,128)}, u32[]{:S(2)}) copy-start(f32[4,64,1024]{2,1,0:T(8,128)} %volume_ref.5) | copy-start | bytes 3145732
  6.1 17.8 %collective-permute-start.1 = (f32[264,1024]{1,0:T(8,128)S(1)}, f32[264,1024]{1,0:T(8,128)S(1)}, u32[]{:S(2)}, u32[]{:S(2)}) collective-permute-start(f32[264,1024]{1,0:T(8,128)S(1)} %pack.1.earlier_ref.own_ref), channel_id=1, source_target_pairs={{1,0},{2,1},{3,2},{4,3},{5,4},{6,5},{7,6},{8,7},{9,8},{10,9},{11,1... | collective-permute-start | bytes 3244040 | tf_op jit(solution)/shard_map/ppermute | solution.py:16
  14.9 4.6 %collective-permute-start = (f32[2,4,4]{2,1,0:T(4,128)S(1)}, f32[2,4,4]{2,1,0:T(4,128)S(1)}, u32[]{:S(2)}, u32[]{:S(2)}) collective-permute-start(f32[2,4,4]{2,1,0:T(4,128)S(1)} %get-tuple-element.7), channel_id=1, source_target_pairs={{0,1},{1,2},{2,3},{3,4},{4,5},{5,6},{6,7},{7,8},{8,9},{9,10},{10,1... | collective-permute-start | bytes 392 | tf_op jit(solution)/shard_map/ppermute | solution.py:16
  17.5 7.9 %collective-permute-start.2 = (f32[4,16,1024]{2,1,0:T(8,128)S(1)}, f32[4,16,1024]{2,1,0:T(8,128)}, u32[]{:S(2)}, u32[]{:S(2)}) collective-permute-start(f32[4,16,1024]{2,1,0:T(8,128)S(1)} %piece.1.piece_ref), channel_id=1, source_target_pairs={{0,1},{1,2},{2,3},{3,4},{4,5},{5,6},{6,7},{7,8},{8,9},{9,10},{10,1... | collective-permute-start | bytes 786440 | tf_op jit(solution)/shard_map/ppermute | solution.py:86
  23.9 1.0 copy-start.4
  25.4 1.2 copy-start.5
  43.5 16.8 %collective-permute-start.4 = (f32[520,128]{1,0:T(8,128)S(1)}, f32[520,128]{1,0:T(8,128)S(1)}, u32[]{:S(2)}, u32[]{:S(2)}) collective-permute-start(f32[520,128]{1,0:T(8,128)S(1)} %gather.1.near_ref), channel_id=1, source_target_pairs={{0,64},{64,0},{128,192},{192,128},{256,320},{320,256},{384,448},{4... | collective-permute-start | bytes 798728 | tf_op jit(solution)/shard_map/ppermute | solution.py:72
  61.7 1.0 copy-start.2
  62.7 34.6 %all-to-all-start.1 = ((f32[4,4,16,1024]{3,2,1,0:T(8,128)}), f32[4,4,16,1024]{3,2,1,0:T(8,128)}, u32[]{:S(2)}, u32[]{:S(2)}) async-start(f32[4,4,16,1024]{3,2,1,0:T(8,128)} %copy-done.2), calls=%async_computation.1 | async-start | bytes 2097152 | tf_op jit(solution)/shard_map/all_to_all | solution.py:53
  68.0 46.8 %copy-start.3 = (f32[4,4,16,1024]{3,2,1,0:T(8,128)S(1)}, f32[4,4,16,1024]{3,2,1,0:T(8,128)}, u32[]{:S(2)}) copy-start(f32[4,4,16,1024]{3,2,1,0:T(8,128)} %copy-done.2) | copy-start | bytes 3145732
  68.0 46.7 %collective-permute-start.3 = (f32[4,64,1024]{2,1,0:T(8,128)}, f32[4,64,1024]{2,1,0:T(8,128)S(1)}, u32[]{:S(2)}, u32[]{:S(2)}) collective-permute-start(f32[4,64,1024]{2,1,0:T(8,128)} %late.1), channel_id=1, source_target_pairs={{0,1},{1,2},{2,3},{3,4},{4,5},{5,6},{6,7},{7,8},{8,9},{9,10},{10,1... | collective-permute-start | bytes 3145736 | tf_op jit(solution)/shard_map/ppermute | solution.py:86
  98.6 20.3 %collective-permute-start.5 = (f32[4,2,16,1024]{3,2,1,0:T(8,128)S(1)}, f32[4,2,16,1024]{3,2,1,0:T(8,128)S(1)}, u32[]{:S(2)}, u32[]{:S(2)}) collective-permute-start(f32[4,2,16,1024]{3,2,1,0:T(8,128)S(1)} %get-tuple-element.11), channel_id=1, source_target_pairs={{0,1},{1,2},{2,3},{3,4},{4,5},{5,6},{6,7},{7,8},{8,9},{9,10},{10,1... | collective-permute-start | bytes 1572872 | tf_op jit(solution)/shard_map/ppermute | solution.py:86
  112.8 10.5 %collective-permute-start.6 = (f32[4,2,16,1024]{3,2,1,0:T(8,128)S(1)}, f32[4,2,16,1024]{3,2,1,0:T(8,128)S(1)}, u32[]{:S(2)}, u32[]{:S(2)}) collective-permute-start(f32[4,2,16,1024]{3,2,1,0:T(8,128)S(1)} %get-tuple-element.10), channel_id=1, source_target_pairs={{1,0},{2,1},{3,2},{4,3},{5,4},{6,5},{7,6},{8,7},{9,8},{10,9},{11,1... | collective-permute-start | bytes 1572872 | tf_op jit(solution)/shard_map/ppermute | solution.py:91

commit v2 on v0

--- a/solution.py
+++ b/solution.py
@@ -108,12 +108,11 @@
     return total
 
 
-def pack_kernel(coef_ref, window_ref, volume_ref, measured_ref, out_ref):
+def pack_kernel(coef_ref, volume_ref, measured_ref, out_ref):
     angles, rows, height, columns = measured_ref.shape
     layers = volume_ref.shape[0]
     depth = 2 * TILE
     coefs = splats(coef_ref)
-    out_ref[angles * rows * height :, :] = window_ref[...]
 
     def chunk(i, carry):
         top = pl.multiple_of(i * depth, depth)
@@ -135,23 +134,23 @@
     lax.fori_loop(0, height // depth, chunk, 0)
 
 
-def pack(coefs, window, volume, measured):
+def pack(coefs, volume, measured):
     angles, rows, height, columns = measured.shape
     return pl.pallas_call(
         pack_kernel,
-        in_specs=[SMEM, VMEM, VMEM, VMEM],
-        out_specs=VMEM,
-        out_shape=jax.ShapeDtypeStruct((angles * rows * height + TILE, columns), jnp.float32),
+        in_specs=[SMEM, VMEM, VMEM],
+        out_specs=VMEM,
+        out_shape=jax.ShapeDtypeStruct((angles * rows * height, columns), jnp.float32),
         compiler_params=pltpu.CompilerParams(vmem_limit_bytes=8 * 2**20),
         name="pack",
-    )(coefs, window, volume, measured)
+    )(coefs, volume, measured)
 
 
 def spread_kernel(coef_ref, sums_ref, own_ref, next_ref, earlier_ref, out_ref):
     count, layers = coef_ref.shape
     ring = out_ref.shape[0]
     columns = own_ref.shape[1]
-    height = (own_ref.shape[0] - TILE) // (count // 2)
+    height = own_ref.shape[0] // (count // 2)
     depth = height // ring
     ytiles, xtiles = depth // TILE, columns // LANES
     coefs = splats(coef_ref)
@@ -213,26 +212,6 @@
         compiler_params=pltpu.CompilerParams(vmem_limit_bytes=8 * 2**20),
         name="gather",
     )(parts)
-
-
-def piece_kernel(place_ref, volume_ref, earlier_ref, out_ref):
-    layers, depth, _ = out_ref.shape
-    top = pl.multiple_of(place_ref[0] * depth, depth)
-    for z in range(layers):
-        out_ref[z] = volume_ref[z, pl.ds(top, depth), :]
-
-
-def piece_of(place, volume, earlier, depth):
-    layers, _, columns = volume.shape
-    return pl.pallas_call(
-        piece_kernel,
-        in_specs=[SMEM, VMEM, ANY],
-        out_specs=VMEM,
-        out_shape=jax.ShapeDtypeStruct((layers, depth, columns), jnp.float32),
-        compiler_params=pltpu.CompilerParams(vmem_limit_bytes=8 * 2**20),
-        cost_estimate=pl.CostEstimate(flops=0, bytes_accessed=32 * 2**20, transcendentals=0),
-        name="piece",
-    )(place, volume, earlier)
 
 
 def late_kernel(volume_ref, earlier_ref, whole_ref):
@@ -294,10 +273,11 @@
     )(coefs, before, own)
 
 
-def update_kernel(near_ref, far_ref, before_ref, piece_ref, out_ref):
+def update_kernel(place_ref, near_ref, far_ref, before_ref, volume_ref, out_ref):
     copies, layers, depth, columns = out_ref.shape
     ytiles, xtiles = depth // TILE, columns // LANES
     body = layers * ytiles * xtiles * TILE
+    top = pl.multiple_of(place_ref[0] * depth, depth)
     sums = near_ref[body:, :] + far_ref[body:, :]
     share = 1.0 / sums[:, 2 * layers : 2 * layers + 1]
     sums = sums * share
@@ -312,25 +292,26 @@
     for t in range(xtiles):
         lanes = pl.ds(t * LANES, LANES)
         for j in range(ytiles):
-            rows = pl.ds(j * TILE, TILE)
-            planes = [ref[z, rows, lanes] for ref in (before_ref, piece_ref) for z in range(layers)]
+            rows = pl.ds(pl.multiple_of(top + j * TILE, TILE), TILE)
+            planes = [ref[z, rows, lanes] for ref in (before_ref, volume_ref) for z in range(layers)]
             for z in range(layers):
                 row = ((z * ytiles + j) * xtiles + t) * TILE
                 total = (near_ref[row : row + TILE, :] + far_ref[row : row + TILE, :]) * shares[z]
                 value = planes[layers + z] + (total - combine(planes, coefs[z]))
                 for copy in range(copies):
-                    out_ref[copy, z, rows, lanes] = value
-
-
-def update(near, far, before, piece, ring):
+                    out_ref[copy, z, pl.ds(j * TILE, TILE), lanes] = value
+
+
+def update(place, near, far, before, volume, ring):
+    layers, height, columns = volume.shape
     return pl.pallas_call(
         update_kernel,
-        in_specs=[VMEM] * 4,
-        out_specs=VMEM,
-        out_shape=jax.ShapeDtypeStruct((ring,) + piece.shape, jnp.float32),
+        in_specs=[SMEM] + [VMEM] * 4,
+        out_specs=VMEM,
+        out_shape=jax.ShapeDtypeStruct((ring, layers, height // ring, columns), jnp.float32),
         compiler_params=pltpu.CompilerParams(vmem_limit_bytes=8 * 2**20),
         name="update",
-    )(near, far, before, piece)
+    )(place, near, far, before, volume)
 
 
 def sweep(source, target, edge, lowest, highest):
@@ -462,37 +443,33 @@
     ).astype(jnp.int32)
 
     window = windows(weights, shifts, bands)
-    low, high = window[:, :own_rows], window[:, own_rows:]
+    low = window[:, :own_rows]
     count = window.shape[0] * own_rows
     flat = lambda block: block.reshape(count, layers)
-    line = jnp.pad(window.reshape(1, -1), ((0, TILE - 1), (0, columns - window.size)))
-    back = pack(flat(low), line, volume, measured)
-    following = from_behind(back, "slab", -1)
     window_before = from_behind(window, "slab", 1)
-    piece = piece_of(place, volume, back, depth)
-    before = to_next(piece)
-    window_after = following[-TILE, : window.size].reshape(window.shape)
-
-    low_after, high_before = window_after[:, :own_rows], window_before[:, own_rows:]
+    back = pack(flat(low), volume, measured)
+    following = to_previous(back)
+    before = to_next(late(volume, back))
+
+    high_before = window_before[:, own_rows:]
     total_own = jnp.sum(low, axis=2) + jnp.sum(high_before, axis=2)
-    total_next = jnp.sum(low_after, axis=2) + jnp.sum(high, axis=2)
-    share_own = 1.0 / jnp.maximum(total_own, 1.0)
-    share_next = jnp.where(slab < last_slab, 1.0 / jnp.maximum(total_next, 1.0), 0.0)
-    coefs_own = flat(low) * share_own.reshape(count, 1)
-    coefs_next = flat(high) * share_next.reshape(count, 1)
+    share_own = (1.0 / jnp.maximum(total_own, 1.0)).reshape(count, 1)
+    coefs_own = flat(low) * share_own
+    arrived = to_previous(
+        jnp.concatenate([flat(high_before) * share_own, flat(high_before)], axis=1)
+    )
+    coefs_next, high_next = arrived[:, :layers], arrived[:, layers:]
     back_coefs = jnp.concatenate([coefs_own, coefs_next])
     normal_before = jnp.sum(coefs_own[:, :, None] * flat(high_before)[:, None, :], axis=0)
-    normal_own = jnp.sum(coefs_next[:, :, None] * flat(high)[:, None, :], axis=0)
+    normal_own = jnp.sum(coefs_next[:, :, None] * high_next[:, None, :], axis=0)
     column_part = jnp.sum(window, axis=(0, 1))
     sums = jnp.concatenate([normal_before, normal_own, column_part[:, None]], axis=1)
     sums = jnp.pad(sums, ((0, TILE - layers), (0, LANES - 2 * layers - 1)))
 
     sent = spread(back_coefs, sums, back, following, before, height, ring)
     near = gather(over_ring(sent))
-    pieces = update(near, from_far(near), before, piece, ring)
-    field = over_ring(pieces)
-    volume_before = to_next(late(volume, pieces))
-    residual, done = residual_of(flat(high_before), volume_before, back, measured.shape)
+    field = over_ring(update(place, near, from_far(near), before, volume, ring))
+    residual, done = residual_of(flat(high_before), before, back, measured.shape)
     halo_low = to_next(field[:, layers - HALO :])
     halo_high = to_previous(field[:, :HALO])
     updated = smooth(place, done, field, halo_low, halo_high)

time: 125 us -> 125 us (level)
  the two profiles are of different devices: /device:TPU:145 before, /device:TPU:81 now
where the time goes in v2:
time: 125 us; the launch traced here: 124 us
  starting transfers between devices  43.1 us (34%)
  blocking collectives  33.8 us (27%)
  waiting for transfers between devices  30.5 us (24%)
  Pallas kernels  11 us (9%)
  local copies, waits for them, and re-layouts  2.59 us (2%)
  between operations  2.08 us (2%)
  other arithmetic  1.46 us (1%)
    all_to_all x2, blocking collectives, over_ring(): lax.all_to_all(pieces, 'ang', split_axis=0, concat_axis=0, axis_index_gro...  33.8 us
    ppermute x2, starting transfers between devices, to_next(): return lax.ppermute(block, ('ang', 'slab'), route(pairs))  21.5 us
    ppermute x1, waiting for transfers between devices, from_far(): lax.ppermute(block, 'ang', [(a, a ^ 1) for a in range(lax.axis_size('ang'...  14.7 us
    ppermute x3, waiting for transfers between devices, to_previous(): return lax.ppermute(block, ('ang', 'slab'), route(pairs))  12.7 us
    ppermute x1, starting transfers between devices, from_far(): lax.ppermute(block, 'ang', [(a, a ^ 1) for a in range(lax.axis_size('ang'...  11.7 us
    ppermute x3, starting transfers between devices, to_previous(): return lax.ppermute(block, ('ang', 'slab'), route(pairs))  5.76 us
    pallas_call x1, Pallas kernels, smooth(): pl.pallas_call(smooth_kernel, in_specs=[SMEM, ANY, VMEM, VMEM, VMEM], out...  4.95 us
    ppermute x1, starting transfers between devices, from_behind(): return lax.ppermute(block, axis, route)  4.11 us
  transfers between devices with their start and end apart: 7, of which 5 were waited for; matrix products, arithmetic and copies ran while one was open for 1% of the time, Pallas kernels for 2%

profile of v2, /device:TPU:81, one launch (start us, length us, event | category | flops | bytes accessed | tf_op | source)
XLA Modules:
  0.0 124.5 jit_solution(16862221348302282046)
XLA Ops:
  2.0 0.8 multiply_reduce_fusion
  2.7 4.1 %collective-permute-start = (f32[2,4,4]{2,1,0:T(4,128)S(1)}, f32[2,4,4]{2,1,0:T(4,128)S(1)}, u32[]{:S(2)}, u32[]{:S(2)}) collective-permute-start(f32[2,4,4]{2,1,0:T(4,128)S(1)} %get-tuple-element.7), channel_id=1, source_target_pairs={{0,1},{1,2},{2,3},{3,4},{4,5},{5,6},{6,7},{7,8},{8,9},{9,10},{10,1... | collective-permute-start | bytes 392 | tf_op jit(solution)/shard_map/ppermute | solution.py:16
  6.9 0.1 slice_reduce_fusion
  6.9 1.2 copy-done
  8.2 1.0 copy-done.2
  9.2 0.9 pack.1.earlier_ref.own_ref
  10.1 1.9 %collective-permute-start.3 = (f32[256,1024]{1,0:T(8,128)S(1)}, f32[256,1024]{1,0:T(8,128)}, u32[]{:S(2)}, u32[]{:S(2)}) collective-permute-start(f32[256,1024]{1,0:T(8,128)S(1)} %pack.1.earlier_ref.own_ref), channel_id=1, source_target_pairs={{1,0},{2,1},{3,2},{4,3},{5,4},{6,5},{7,6},{8,7},{9,8},{10,9},{11,1... | collective-permute-start | bytes 3145736 | tf_op jit(solution)/shard_map/ppermute | solution.py:91
  12.1 3.6 %collective-permute-start.1 = (f32[4,64,1024]{2,1,0:T(8,128)S(1)}, f32[4,64,1024]{2,1,0:T(8,128)S(1)}, u32[]{:S(2)}, u32[]{:S(2)}) collective-permute-start(f32[4,64,1024]{2,1,0:T(8,128)S(1)} %late.1), channel_id=1, source_target_pairs={{0,1},{1,2},{2,3},{3,4},{4,5},{5,6},{6,7},{7,8},{8,9},{9,10},{10,1... | collective-permute-start | bytes 3145736 | tf_op jit(solution)/shard_map/ppermute | solution.py:86
  15.8 0.1 copy.8
  15.9 0.1 slice_reduce_fusion.1
  16.0 0.1 div.22
  16.1 0.1 pad_maximum_fusion.1
  16.2 1.9 %collective-permute-start.2 = (f32[4,8]{1,0:T(4,128)S(1)}, f32[4,8]{1,0:T(4,128)S(1)}, u32[]{:S(2)}, u32[]{:S(2)}) collective-permute-start(f32[4,8]{1,0:T(4,128)S(1)} %pad_maximum_fusion.1), channel_id=1, source_target_pairs={{1,0},{2,1},{3,2},{4,3},{5,4},{6,5},{7,6},{8,7},{9,8},{10,9},{11,1... | collective-permute-start | bytes 392 | tf_op jit(solution)/shard_map/ppermute | solution.py:91
  18.1 0.1 multiply_reduce_fusion.3
  18.2 8.3 %collective-permute-done.2 = f32[4,8]{1,0:T(4,128)S(1)} collective-permute-done((f32[4,8]{1,0:T(4,128)S(1)}, f32[4,8]{1,0:T(4,128)S(1)}, u32[]{:S(2)}, u32[]{:S(2)}) %collective-permute-start.2) | collective-permute-done | bytes 160 | tf_op jit(solution)/shard_map/ppermute | solution.py:91
  26.6 0.1 multiply_reduce_fusion.2
  26.7 0.1 select_maximum_fusion.sums_ref
  26.8 0.7 collective-permute-done.1.before_ref.earlier_ref
  27.5 1.8 %spread.1 = f32[4,520,128]{2,1,0:T(8,128)S(1)} custom-call(f32[8,4]{1,0:T(8,128)S(1)} %pad_maximum_fusion.coef_ref, f32[8,128]{1,0:T(8,128)S(1)} %select_maximum_fusion.sums_ref, f32[256,1024]{1,0:T(8,128)S(1)} %pack.1.earlier_ref.own_ref, f32[256,1024]{1,0:T(8,128)} %collective-permute-done.3.next_ref, ...), custom_call_target="tpu_custom_call" | custom-call | tf_op jit(solution)/shard_map/spread/pallas_call | solution.py:181
  29.3 17.9 %all_to_all.10.parts_ref = f32[4,520,128]{2,1,0:T(8,128)S(1)} all-to-all(f32[4,520,128]{2,1,0:T(8,128)S(1)} %spread.1), channel_id=1, replica_groups={{0,128,256,384},{64,192,320,448},{1,129,257,385},{65,193,321,449},{2,13..., dimensions={0} | all-to-all | bytes 2129920 | tf_op jit(solution)/shard_map/all_to_all | solution.py:53
  47.2 0.1 gather.1.near_ref
  47.3 11.7 %collective-permute-start.4 = (f32[520,128]{1,0:T(8,128)S(1)}, f32[520,128]{1,0:T(8,128)}, u32[]{:S(2)}, u32[]{:S(2)}) collective-permute-start(f32[520,128]{1,0:T(8,128)S(1)} %gather.1.near_ref), channel_id=1, source_target_pairs={{0,64},{64,0},{128,192},{192,128},{256,320},{320,256},{384,448},{4... | collective-permute-start | bytes 798728 | tf_op jit(solution)/shard_map/ppermute | solution.py:72
  59.0 0.1 pad_add_fusion.place_ref
  59.1 14.7 %collective-permute-done.4.far_ref = f32[520,128]{1,0:T(8,128)} collective-permute-done((f32[520,128]{1,0:T(8,128)S(1)}, f32[520,128]{1,0:T(8,128)}, u32[]{:S(2)}, u32[]{:S(2)}) %collective-permute-start.4) | collective-permute-done | bytes 266272 | tf_op jit(solution)/shard_map/ppermute | solution.py:72
  73.8 1.3 %update.1 = f32[4,4,16,1024]{3,2,1,0:T(8,128)S(1)} custom-call(s32[3]{0:T(128)S(1)} %pad_add_fusion.place_ref, f32[520,128]{1,0:T(8,128)S(1)} %gather.1.near_ref, f32[520,128]{1,0:T(8,128)} %collective-permute-done.4.far_ref, f32[4,64,1024]{2,1,0:T(8,128)S(1)} %collective-permute-done.1.before_ref.earlier_ref, f32[4,64,1024]{2,1,0:T(8,128)S(1)} %copy-done.1), custom_call_target="tpu_custom_call" | custom-call | tf_op jit(solution)/shard_map/update/pallas_call | solution.py:307
  75.1 16.0 %all_to_all.11.own_ref = f32[4,4,16,1024]{3,2,1,0:T(8,128)S(1)} all-to-all(f32[4,4,16,1024]{3,2,1,0:T(8,128)S(1)} %update.1), channel_id=1, replica_groups={{0,128,256,384},{64,192,320,448},{1,129,257,385},{65,193,321,449},{2,13..., dimensions={0} | all-to-all | bytes 2097152 | tf_op jit(solution)/shard_map/all_to_all | solution.py:53
  91.2 17.9 %collective-permute-start.5 = (f32[4,2,16,1024]{3,2,1,0:T(8,128)S(1)}, f32[4,2,16,1024]{3,2,1,0:T(8,128)S(1)}, u32[]{:S(2)}, u32[]{:S(2)}) collective-permute-start(f32[4,2,16,1024]{3,2,1,0:T(8,128)S(1)} %get-tuple-element.9), channel_id=1, source_target_pairs={{0,1},{1,2},{2,3},{3,4},{4,5},{5,6},{6,7},{7,8},{8,9},{9,10},{10,1... | collective-permute-start | bytes 1572872 | tf_op jit(solution)/shard_map/ppermute | solution.py:86
  109.0 1.9 %collective-permute-start.6 = (f32[4,2,16,1024]{3,2,1,0:T(8,128)S(1)}, f32[4,2,16,1024]{3,2,1,0:T(8,128)S(1)}, u32[]{:S(2)}, u32[]{:S(2)}) collective-permute-start(f32[4,2,16,1024]{3,2,1,0:T(8,128)S(1)} %get-tuple-element.8), channel_id=1, source_target_pairs={{1,0},{2,1},{3,2},{4,3},{5,4},{6,5},{7,6},{8,7},{9,8},{10,9},{11,1... | collective-permute-start | bytes 1572872 | tf_op jit(solution)/shard_map/ppermute | solution.py:91
  111.0 1.8 %residual.1 = (f32[2,2,64,1024]{3,2,1,0:T(8,128)}, f32[8,128]{1,0:T(8,128)S(1)}) custom-call(f32[4,4]{1,0:T(4,128)S(1)} %bitcast.13, f32[4,64,1024]{2,1,0:T(8,128)S(1)} %collective-permute-done.1.before_ref.earlier_ref, f32[256,1024]{1,0:T(8,128)S(1)} %pack.1.earlier_ref.own_ref), custom_call_target="tpu_custom_call" | custom-call | bytes 16777216 | tf_op jit(solution)/shard_map/residual/pallas_call | solution.py:262
  112.8 2.3 %collective-permute-done.5.low_ref = f32[4,2,16,1024]{3,2,1,0:T(8,128)S(1)} collective-permute-done((f32[4,2,16,1024]{3,2,1,0:T(8,128)S(1)}, f32[4,2,16,1024]{3,2,1,0:T(8,128)S(1)}, u32[]{:S(2)}, u32[]{:S(2)}) %collective-permute-start.5) | collective-permute-done | bytes 524320 | tf_op jit(solution)/shard_map/ppermute | solution.py:86
  115.1 4.4 %collective-permute-done.6.high_ref = f32[4,2,16,1024]{3,2,1,0:T(8,128)S(1)} collective-permute-done((f32[4,2,16,1024]{3,2,1,0:T(8,128)S(1)}, f32[4,2,16,1024]{3,2,1,0:T(8,128)S(1)}, u32[]{:S(2)}, u32[]{:S(2)}) %collective-permute-start.6) | collective-permute-done | bytes 524320 | tf_op jit(solution)/shard_map/ppermute | solution.py:91
  119.5 5.0 %smooth.1 = f32[4,64,1024]{2,1,0:T(8,128)} custom-call(s32[3]{0:T(128)S(1)} %pad_add_fusion.place_ref, f32[8,128]{1,0:T(8,128)S(1)} %get-tuple-element.4.earlier_ref, f32[4,4,16,1024]{3,2,1,0:T(8,128)S(1)} %all_to_all.11.own_ref, f32[4,2,16,1024]{3,2,1,0:T(8,128)S(1)} %collective-permute-done.5.low_ref, f32[4,2,16,1024]{3,2,1,0:T(8,128)S(1)} %collective-permute-done.6.high_ref), custom_call_target="tpu_custom_call" | custom-call | tf_op jit(solution)/shard_map/smooth/pallas_call | solution.py:411
  (15 shorter events, 0.3 us)
Async XLA Ops:
  2.7 13.1 %collective-permute-start = (f32[2,4,4]{2,1,0:T(4,128)S(1)}, f32[2,4,4]{2,1,0:T(4,128)S(1)}, u32[]{:S(2)}, u32[]{:S(2)}) collective-permute-start(f32[2,4,4]{2,1,0:T(4,128)S(1)} %get-tuple-element.7), channel_id=1, source_target_pairs={{0,1},{1,2},{2,3},{3,4},{4,5},{5,6},{6,7},{7,8},{8,9},{9,10},{10,1... | collective-permute-start | bytes 392 | tf_op jit(solution)/shard_map/ppermute | solution.py:16
  6.9 1.2 copy-start
  8.2 1.0 copy-start.2
  10.1 17.4 %collective-permute-start.3 = (f32[256,1024]{1,0:T(8,128)S(1)}, f32[256,1024]{1,0:T(8,128)}, u32[]{:S(2)}, u32[]{:S(2)}) collective-permute-start(f32[256,1024]{1,0:T(8,128)S(1)} %pack.1.earlier_ref.own_ref), channel_id=1, source_target_pairs={{1,0},{2,1},{3,2},{4,3},{5,4},{6,5},{7,6},{8,7},{9,8},{10,9},{11,1... | collective-permute-start | bytes 3145736 | tf_op jit(solution)/shard_map/ppermute | solution.py:91
  12.1 15.4 %collective-permute-start.1 = (f32[4,64,1024]{2,1,0:T(8,128)S(1)}, f32[4,64,1024]{2,1,0:T(8,128)S(1)}, u32[]{:S(2)}, u32[]{:S(2)}) collective-permute-start(f32[4,64,1024]{2,1,0:T(8,128)S(1)} %late.1), channel_id=1, source_target_pairs={{0,1},{1,2},{2,3},{3,4},{4,5},{5,6},{6,7},{7,8},{8,9},{9,10},{10,1... | collective-permute-start | bytes 3145736 | tf_op jit(solution)/shard_map/ppermute | solution.py:86
  16.2 10.3 %collective-permute-start.2 = (f32[4,8]{1,0:T(4,128)S(1)}, f32[4,8]{1,0:T(4,128)S(1)}, u32[]{:S(2)}, u32[]{:S(2)}) collective-permute-start(f32[4,8]{1,0:T(4,128)S(1)} %pad_maximum_fusion.1), channel_id=1, source_target_pairs={{1,0},{2,1},{3,2},{4,3},{5,4},{6,5},{7,6},{8,7},{9,8},{10,9},{11,1... | collective-permute-start | bytes 392 | tf_op jit(solution)/shard_map/ppermute | solution.py:91
  47.2 26.6 %copy-start.1 = (f32[4,64,1024]{2,1,0:T(8,128)S(1)}, f32[4,64,1024]{2,1,0:T(8,128)}, u32[]{:S(2)}) copy-start(f32[4,64,1024]{2,1,0:T(8,128)} %volume_ref.5) | copy-start | bytes 3145732
  47.3 26.5 %collective-permute-start.4 = (f32[520,128]{1,0:T(8,128)S(1)}, f32[520,128]{1,0:T(8,128)}, u32[]{:S(2)}, u32[]{:S(2)}) collective-permute-start(f32[520,128]{1,0:T(8,128)S(1)} %gather.1.near_ref), channel_id=1, source_target_pairs={{0,64},{64,0},{128,192},{192,128},{256,320},{320,256},{384,448},{4... | collective-permute-start | bytes 798728 | tf_op jit(solution)/shard_map/ppermute | solution.py:72
  91.2 24.0 %collective-permute-start.5 = (f32[4,2,16,1024]{3,2,1,0:T(8,128)S(1)}, f32[4,2,16,1024]{3,2,1,0:T(8,128)S(1)}, u32[]{:S(2)}, u32[]{:S(2)}) collective-permute-start(f32[4,2,16,1024]{3,2,1,0:T(8,128)S(1)} %get-tuple-element.9), channel_id=1, source_target_pairs={{0,1},{1,2},{2,3},{3,4},{4,5},{5,6},{6,7},{7,8},{8,9},{9,10},{10,1... | collective-permute-start | bytes 1572872 | tf_op jit(solution)/shard_map/ppermute | solution.py:86
  109.0 10.5 %collective-permute-start.6 = (f32[4,2,16,1024]{3,2,1,0:T(8,128)S(1)}, f32[4,2,16,1024]{3,2,1,0:T(8,128)S(1)}, u32[]{:S(2)}, u32[]{:S(2)}) collective-permute-start(f32[4,2,16,1024]{3,2,1,0:T(8,128)S(1)} %get-tuple-element.8), channel_id=1, source_target_pairs={{1,0},{2,1},{3,2},{4,3},{5,4},{6,5},{7,6},{8,7},{9,8},{10,9},{11,1... | collective-permute-start | bytes 1572872 | tf_op jit(solution)/shard_map/ppermute | solution.py:91

commit v3 on v2

--- a/solution.py
+++ b/solution.py
@@ -44,6 +44,13 @@
     return lax.ppermute(block, "ang", [(a, a ^ 1) for a in range(lax.axis_size("ang"))])
 
 
+def from_far_at_row_ends(block):
+    count, slabs = lax.axis_size("ang"), lax.axis_size("slab")
+    ends = range(ROW - 1, slabs, ROW)
+    pairs = [(a * slabs + t, (a ^ 1) * slabs + t) for a in range(count) for t in ends]
+    return lax.ppermute(block, ("ang", "slab"), pairs)
+
+
 def to_next(block):
     pairs = [(s, s + 1) for s in range(lax.axis_size("slab"))]
     return lax.ppermute(block, ("ang", "slab"), route(pairs))
@@ -81,6 +88,13 @@
     return lax.ppermute(block, ("ang", "slab"), route(pairs))
 
 
+def from_far_at_row_ends(block):
+    count, slabs = lax.axis_size("ang"), lax.axis_size("slab")
+    ends = range(ROW - 1, slabs, ROW)
+    pairs = [(a * slabs + t, (a ^ 1) * slabs + t) for a in range(count) for t in ends]
+    return lax.ppermute(block, ("ang", "slab"), pairs)
+
+
 def to_next(block):
     pairs = [(s, s + 1) for s in range(lax.axis_size("slab"))]
     return lax.ppermute(block, ("ang", "slab"), route(pairs))
@@ -108,11 +122,12 @@
     return total
 
 
-def pack_kernel(coef_ref, volume_ref, measured_ref, out_ref):
+def pack_kernel(coef_ref, window_ref, volume_ref, measured_ref, out_ref):
     angles, rows, height, columns = measured_ref.shape
     layers = volume_ref.shape[0]
     depth = 2 * TILE
     coefs = splats(coef_ref)
+    out_ref[angles * rows * height :, :] = window_ref[...]
 
     def chunk(i, carry):
         top = pl.multiple_of(i * depth, depth)
@@ -134,23 +149,23 @@
     lax.fori_loop(0, height // depth, chunk, 0)
 
 
-def pack(coefs, volume, measured):
+def pack(coefs, window, volume, measured):
     angles, rows, height, columns = measured.shape
     return pl.pallas_call(
         pack_kernel,
-        in_specs=[SMEM, VMEM, VMEM],
+        in_specs=[SMEM, VMEM, VMEM, VMEM],
         out_specs=VMEM,
-        out_shape=jax.ShapeDtypeStruct((angles * rows * height, columns), jnp.float32),
+        out_shape=jax.ShapeDtypeStruct((angles * rows * height + TILE, columns), jnp.float32),
         compiler_params=pltpu.CompilerParams(vmem_limit_bytes=8 * 2**20),
         name="pack",
-    )(coefs, volume, measured)
+    )(coefs, window, volume, measured)
 
 
 def spread_kernel(coef_ref, sums_ref, own_ref, next_ref, earlier_ref, out_ref):
     count, layers = coef_ref.shape
     ring = out_ref.shape[0]
     columns = own_ref.shape[1]
-    height = own_ref.shape[0] // (count // 2)
+    height = (own_ref.shape[0] - TILE) // (count // 2)
     depth = height // ring
     ytiles, xtiles = depth // TILE, columns // LANES
     coefs = splats(coef_ref)
@@ -214,21 +229,25 @@
     )(parts)
 
 
-def late_kernel(volume_ref, earlier_ref, whole_ref):
+def late_kernel(volume_ref, window_ref, earlier_ref, whole_ref, window_out_ref):
+    window_out_ref[...] = window_ref[...]
     for z in range(volume_ref.shape[0]):
         whole_ref[z] = volume_ref[z]
 
 
-def late(volume, earlier):
+def late(volume, window, earlier):
     return pl.pallas_call(
         late_kernel,
-        in_specs=[VMEM, ANY],
-        out_specs=VMEM,
-        out_shape=jax.ShapeDtypeStruct(volume.shape, jnp.float32),
+        in_specs=[VMEM, VMEM, ANY],
+        out_specs=[VMEM, VMEM],
+        out_shape=[
+            jax.ShapeDtypeStruct(volume.shape, jnp.float32),
+            jax.ShapeDtypeStruct(window.shape, jnp.float32),
+        ],
         compiler_params=pltpu.CompilerParams(vmem_limit_bytes=8 * 2**20),
         cost_estimate=pl.CostEstimate(flops=0, bytes_accessed=32 * 2**20, transcendentals=0),
         name="late",
-    )(volume, earlier)
+    )(volume, window, earlier)
 
 
 def residual_kernel(coef_ref, before_ref, own_ref, out_ref, done_ref):
@@ -446,22 +465,26 @@
     low = window[:, :own_rows]
     count = window.shape[0] * own_rows
     flat = lambda block: block.reshape(count, layers)
+    line = jnp.pad(window.reshape(1, -1), ((0, TILE - 1), (0, columns - window.size)))
+    back = pack(flat(low), line, volume, measured)
+    following = to_previous(back)
     window_before = from_behind(window, "slab", 1)
-    back = pack(flat(low), volume, measured)
-    following = to_previous(back)
-    before = to_next(late(volume, back))
-
-    high_before = window_before[:, own_rows:]
+    whole, window_late = late(volume, window, back)
+    before = to_next(whole)
+    other = from_far_at_row_ends(window_late)
+    high_next = jnp.where(slab % ROW == ROW - 1, other, window)[:, own_rows:]
+
+    window_after = following[-TILE, : window.size].reshape(window.shape)
+    low_after, high_before = window_after[:, :own_rows], window_before[:, own_rows:]
     total_own = jnp.sum(low, axis=2) + jnp.sum(high_before, axis=2)
-    share_own = (1.0 / jnp.maximum(total_own, 1.0)).reshape(count, 1)
-    coefs_own = flat(low) * share_own
-    arrived = to_previous(
-        jnp.concatenate([flat(high_before) * share_own, flat(high_before)], axis=1)
-    )
-    coefs_next, high_next = arrived[:, :layers], arrived[:, layers:]
+    total_next = jnp.sum(low_after, axis=2) + jnp.sum(high_next, axis=2)
+    share_own = 1.0 / jnp.maximum(total_own, 1.0)
+    share_next = jnp.where(slab < last_slab, 1.0 / jnp.maximum(total_next, 1.0), 0.0)
+    coefs_own = flat(low) * share_own.reshape(count, 1)
+    coefs_next = flat(high_next) * share_next.reshape(count, 1)
     back_coefs = jnp.concatenate([coefs_own, coefs_next])
     normal_before = jnp.sum(coefs_own[:, :, None] * flat(high_before)[:, None, :], axis=0)
-    normal_own = jnp.sum(coefs_next[:, :, None] * high_next[:, None, :], axis=0)
+    normal_own = jnp.sum(coefs_next[:, :, None] * flat(high_next)[:, None, :], axis=0)
     column_part = jnp.sum(window, axis=(0, 1))
     sums = jnp.concatenate([normal_before, normal_own, column_part[:, None]], axis=1)
     sums = jnp.pad(sums, ((0, TILE - layers), (0, LANES - 2 * layers - 1)))

time: 125 us -> 126 us (level)
  the two profiles are of different devices: /device:TPU:81 before, /device:TPU:89 now
where the time goes in v3:
time: 126 us; the launch traced here: 125 us
  starting transfers between devices  54.5 us (43%)
  blocking collectives  30.1 us (24%)
  waiting for transfers between devices  21.6 us (17%)
  Pallas kernels  12 us (10%)
  local copies, waits for them, and re-layouts  3.47 us (3%)
  between operations  2.11 us (2%)
  other arithmetic  1.55 us (1%)
    ppermute x2, starting transfers between devices, to_next(): return lax.ppermute(block, ('ang', 'slab'), route(pairs))  34.2 us
    all_to_all x2, blocking collectives, over_ring(): lax.all_to_all(pieces, 'ang', split_axis=0, concat_axis=0, axis_index_gro...  30.1 us
    ppermute x1, starting transfers between devices, from_far(): lax.ppermute(block, 'ang', [(a, a ^ 1) for a in range(lax.axis_size('ang'...  11.7 us
    ppermute x2, waiting for transfers between devices, to_previous(): return lax.ppermute(block, ('ang', 'slab'), route(pairs))  11.2 us
    ppermute x2, waiting for transfers between devices, to_next(): return lax.ppermute(block, ('ang', 'slab'), route(pairs))  5.85 us
    pallas_call x1, Pallas kernels, smooth(): pl.pallas_call(smooth_kernel, in_specs=[SMEM, ANY, VMEM, VMEM, VMEM], out...  4.95 us
    ppermute x1, waiting for transfers between devices, from_far(): lax.ppermute(block, 'ang', [(a, a ^ 1) for a in range(lax.axis_size('ang'...  4.59 us
    ppermute x2, starting transfers between devices, to_previous(): return lax.ppermute(block, ('ang', 'slab'), route(pairs))  4.51 us
  transfers between devices with their start and end apart: 7, of which 5 were waited for; matrix products, arithmetic and copies ran while one was open for 1% of the time, Pallas kernels for 2%

profile of v3, /device:TPU:89, one launch (start us, length us, event | category | flops | bytes accessed | tf_op | source)
XLA Modules:
  0.0 125.3 jit_solution(13788899151547356490)
XLA Ops:
  2.0 0.8 multiply_reduce_fusion
  2.8 0.1 reshape.147
  2.9 1.2 copy-done
  4.1 1.0 copy-done.2
  5.1 0.9 pack.1.earlier_ref.own_ref
  6.0 2.6 %collective-permute-start.3 = (f32[264,1024]{1,0:T(8,128)S(1)}, f32[264,1024]{1,0:T(8,128)}, u32[]{:S(2)}, u32[]{:S(2)}) collective-permute-start(f32[264,1024]{1,0:T(8,128)S(1)} %pack.1.earlier_ref.own_ref), channel_id=1, source_target_pairs={{1,0},{2,1},{3,2},{4,3},{5,4},{6,5},{7,6},{8,7},{9,8},{10,9},{11,1... | collective-permute-start | bytes 3244040 | tf_op jit(solution)/shard_map/ppermute | solution.py:105
  8.6 3.4 %collective-permute-start = (f32[2,4,4]{2,1,0:T(4,128)S(1)}, f32[2,4,4]{2,1,0:T(4,128)S(1)}, u32[]{:S(2)}, u32[]{:S(2)}) collective-permute-start(f32[2,4,4]{2,1,0:T(4,128)S(1)} %get-tuple-element.11.window_ref), channel_id=1, source_target_pairs={{0,1},{1,2},{2,3},{3,4},{4,5},{5,6},{6,7},{7,8},{8,9},{9,10},{10,1... | collective-permute-start | bytes 392 | tf_op jit(solution)/shard_map/ppermute | solution.py:16
  12.1 1.0 late.1
  13.1 0.6 collective-permute-start.2
  13.8 2.4 %collective-permute-start.1 = (f32[4,64,1024]{2,1,0:T(8,128)}, f32[4,64,1024]{2,1,0:T(8,128)S(1)}, u32[]{:S(2)}, u32[]{:S(2)}) collective-permute-start(f32[4,64,1024]{2,1,0:T(8,128)} %get-tuple-element.6), channel_id=1, source_target_pairs={{0,1},{1,2},{2,3},{3,4},{4,5},{5,6},{6,7},{7,8},{8,9},{9,10},{10,1... | collective-permute-start | bytes 3145736 | tf_op jit(solution)/shard_map/ppermute | solution.py:100
  16.2 0.1 copy.8
  16.3 0.1 slice_reduce_fusion.3
  16.4 0.1 fusion.2
  16.5 6.8 %collective-permute-done.3.next_ref = f32[264,1024]{1,0:T(8,128)} collective-permute-done((f32[264,1024]{1,0:T(8,128)S(1)}, f32[264,1024]{1,0:T(8,128)}, u32[]{:S(2)}, u32[]{:S(2)}) %collective-permute-start.3) | collective-permute-done | bytes 1081376 | tf_op jit(solution)/shard_map/ppermute | solution.py:105
  23.3 0.7 slice_reduce_fusion.1
  23.9 0.1 reshape_squeeze.3
  24.0 0.1 slice_reduce_fusion
  24.1 0.1 div.30
  24.7 3.5 %collective-permute-done.1.before_ref.earlier_ref = f32[4,64,1024]{2,1,0:T(8,128)S(1)} collective-permute-done((f32[4,64,1024]{2,1,0:T(8,128)}, f32[4,64,1024]{2,1,0:T(8,128)S(1)}, u32[]{:S(2)}, u32[]{:S(2)}) %collective-permute-start.1) | collective-permute-done | bytes 1048608 | tf_op jit(solution)/shard_map/ppermute | solution.py:100
  28.2 1.8 %spread.1 = f32[4,520,128]{2,1,0:T(8,128)S(1)} custom-call(f32[8,4]{1,0:T(8,128)S(1)} %pad_maximum_fusion.coef_ref, f32[8,128]{1,0:T(8,128)S(1)} %select_maximum_fusion.sums_ref, f32[264,1024]{1,0:T(8,128)S(1)} %pack.1.earlier_ref.own_ref, f32[264,1024]{1,0:T(8,128)} %collective-permute-done.3.next_ref, ...), custom_call_target="tpu_custom_call" | custom-call | tf_op jit(solution)/shard_map/spread/pallas_call | solution.py:196
  30.0 18.0 %all_to_all.10.parts_ref = f32[4,520,128]{2,1,0:T(8,128)S(1)} all-to-all(f32[4,520,128]{2,1,0:T(8,128)S(1)} %spread.1), channel_id=1, replica_groups={{0,128,256,384},{64,192,320,448},{1,129,257,385},{65,193,321,449},{2,13..., dimensions={0} | all-to-all | bytes 2129920 | tf_op jit(solution)/shard_map/all_to_all | solution.py:60
  48.0 0.1 gather.1.near_ref
  48.1 11.7 %collective-permute-start.4 = (f32[520,128]{1,0:T(8,128)S(1)}, f32[520,128]{1,0:T(8,128)}, u32[]{:S(2)}, u32[]{:S(2)}) collective-permute-start(f32[520,128]{1,0:T(8,128)S(1)} %gather.1.near_ref), channel_id=1, source_target_pairs={{0,64},{64,0},{128,192},{192,128},{256,320},{320,256},{384,448},{4... | collective-permute-start | bytes 798728 | tf_op jit(solution)/shard_map/ppermute | solution.py:79
  59.9 4.6 %collective-permute-done.4.far_ref = f32[520,128]{1,0:T(8,128)} collective-permute-done((f32[520,128]{1,0:T(8,128)S(1)}, f32[520,128]{1,0:T(8,128)}, u32[]{:S(2)}, u32[]{:S(2)}) %collective-permute-start.4) | collective-permute-done | bytes 266272 | tf_op jit(solution)/shard_map/ppermute | solution.py:79
  64.5 1.3 %update.1 = f32[4,4,16,1024]{3,2,1,0:T(8,128)S(1)} custom-call(s32[3]{0:T(128)S(1)} %pad_add_fusion.place_ref, f32[520,128]{1,0:T(8,128)S(1)} %gather.1.near_ref, f32[520,128]{1,0:T(8,128)} %collective-permute-done.4.far_ref, f32[4,64,1024]{2,1,0:T(8,128)S(1)} %collective-permute-done.1.before_ref.earlier_ref, f32[4,64,1024]{2,1,0:T(8,128)S(1)} %copy-done.1), custom_call_target="tpu_custom_call" | custom-call | tf_op jit(solution)/shard_map/update/pallas_call | solution.py:326
  65.9 12.2 %all_to_all.11.own_ref = f32[4,4,16,1024]{3,2,1,0:T(8,128)S(1)} all-to-all(f32[4,4,16,1024]{3,2,1,0:T(8,128)S(1)} %update.1), channel_id=1, replica_groups={{0,128,256,384},{64,192,320,448},{1,129,257,385},{65,193,321,449},{2,13..., dimensions={0} | all-to-all | bytes 2097152 | tf_op jit(solution)/shard_map/all_to_all | solution.py:60
  78.1 31.8 %collective-permute-start.5 = (f32[4,2,16,1024]{3,2,1,0:T(8,128)S(1)}, f32[4,2,16,1024]{3,2,1,0:T(8,128)S(1)}, u32[]{:S(2)}, u32[]{:S(2)}) collective-permute-start(f32[4,2,16,1024]{3,2,1,0:T(8,128)S(1)} %get-tuple-element.15), channel_id=1, source_target_pairs={{0,1},{1,2},{2,3},{3,4},{4,5},{5,6},{6,7},{7,8},{8,9},{9,10},{10,1... | collective-permute-start | bytes 1572872 | tf_op jit(solution)/shard_map/ppermute | solution.py:100
  109.9 1.9 %collective-permute-start.6 = (f32[4,2,16,1024]{3,2,1,0:T(8,128)S(1)}, f32[4,2,16,1024]{3,2,1,0:T(8,128)S(1)}, u32[]{:S(2)}, u32[]{:S(2)}) collective-permute-start(f32[4,2,16,1024]{3,2,1,0:T(8,128)S(1)} %get-tuple-element.14), channel_id=1, source_target_pairs={{1,0},{2,1},{3,2},{4,3},{5,4},{6,5},{7,6},{8,7},{9,8},{10,9},{11,1... | collective-permute-start | bytes 1572872 | tf_op jit(solution)/shard_map/ppermute | solution.py:105
  111.8 1.8 %residual.1 = (f32[2,2,64,1024]{3,2,1,0:T(8,128)}, f32[8,128]{1,0:T(8,128)S(1)}) custom-call(f32[4,4]{1,0:T(4,128)S(1)} %bitcast.12, f32[4,64,1024]{2,1,0:T(8,128)S(1)} %collective-permute-done.1.before_ref.earlier_ref, f32[264,1024]{1,0:T(8,128)S(1)} %pack.1.earlier_ref.own_ref), custom_call_target="tpu_custom_call" | custom-call | bytes 16777216 | tf_op jit(solution)/shard_map/residual/pallas_call | solution.py:281
  113.7 2.3 %collective-permute-done.5.low_ref = f32[4,2,16,1024]{3,2,1,0:T(8,128)S(1)} collective-permute-done((f32[4,2,16,1024]{3,2,1,0:T(8,128)S(1)}, f32[4,2,16,1024]{3,2,1,0:T(8,128)S(1)}, u32[]{:S(2)}, u32[]{:S(2)}) %collective-permute-start.5) | collective-permute-done | bytes 524320 | tf_op jit(solution)/shard_map/ppermute | solution.py:100
  116.0 4.4 %collective-permute-done.6.high_ref = f32[4,2,16,1024]{3,2,1,0:T(8,128)S(1)} collective-permute-done((f32[4,2,16,1024]{3,2,1,0:T(8,128)S(1)}, f32[4,2,16,1024]{3,2,1,0:T(8,128)S(1)}, u32[]{:S(2)}, u32[]{:S(2)}) %collective-permute-start.6) | collective-permute-done | bytes 524320 | tf_op jit(solution)/shard_map/ppermute | solution.py:105
  120.4 5.0 %smooth.1 = f32[4,64,1024]{2,1,0:T(8,128)} custom-call(s32[3]{0:T(128)S(1)} %pad_add_fusion.place_ref, f32[8,128]{1,0:T(8,128)S(1)} %get-tuple-element.7.earlier_ref, f32[4,4,16,1024]{3,2,1,0:T(8,128)S(1)} %all_to_all.11.own_ref, f32[4,2,16,1024]{3,2,1,0:T(8,128)S(1)} %collective-permute-done.5.low_ref, f32[4,2,16,1024]{3,2,1,0:T(8,128)S(1)} %collective-permute-done.6.high_ref), custom_call_target="tpu_custom_call" | custom-call | tf_op jit(solution)/shard_map/smooth/pallas_call | solution.py:430
  (21 shorter events, 0.7 us)
Async XLA Ops:
  2.8 1.2 copy-start
  4.1 1.0 copy-start.2
  6.0 17.2 %collective-permute-start.3 = (f32[264,1024]{1,0:T(8,128)S(1)}, f32[264,1024]{1,0:T(8,128)}, u32[]{:S(2)}, u32[]{:S(2)}) collective-permute-start(f32[264,1024]{1,0:T(8,128)S(1)} %pack.1.earlier_ref.own_ref), channel_id=1, source_target_pairs={{1,0},{2,1},{3,2},{4,3},{5,4},{6,5},{7,6},{8,7},{9,8},{10,9},{11,1... | collective-permute-start | bytes 3244040 | tf_op jit(solution)/shard_map/ppermute | solution.py:105
  8.6 7.7 %collective-permute-start = (f32[2,4,4]{2,1,0:T(4,128)S(1)}, f32[2,4,4]{2,1,0:T(4,128)S(1)}, u32[]{:S(2)}, u32[]{:S(2)}) collective-permute-start(f32[2,4,4]{2,1,0:T(4,128)S(1)} %get-tuple-element.11.window_ref), channel_id=1, source_target_pairs={{0,1},{1,2},{2,3},{3,4},{4,5},{5,6},{6,7},{7,8},{8,9},{9,10},{10,1... | collective-permute-start | bytes 392 | tf_op jit(solution)/shard_map/ppermute | solution.py:16
  13.1 3.3 %collective-permute-start.2 = (f32[2,4,4]{2,1,0:T(4,128)S(1)}, f32[2,4,4]{2,1,0:T(4,128)S(1)}, u32[]{:S(2)}, u32[]{:S(2)}) collective-permute-start(f32[2,4,4]{2,1,0:T(4,128)S(1)} %get-tuple-element.8), channel_id=1, source_target_pairs={{15,79},{31,95},{47,111},{63,127},{79,15},{95,31},{111,47},{127,63... | collective-permute-start | bytes 392 | tf_op jit(solution)/shard_map/ppermute | solution.py:95
  13.8 14.5 %collective-permute-start.1 = (f32[4,64,1024]{2,1,0:T(8,128)}, f32[4,64,1024]{2,1,0:T(8,128)S(1)}, u32[]{:S(2)}, u32[]{:S(2)}) collective-permute-start(f32[4,64,1024]{2,1,0:T(8,128)} %get-tuple-element.6), channel_id=1, source_target_pairs={{0,1},{1,2},{2,3},{3,4},{4,5},{5,6},{6,7},{7,8},{8,9},{9,10},{10,1... | collective-permute-start | bytes 3145736 | tf_op jit(solution)/shard_map/ppermute | solution.py:100
  48.0 16.5 %copy-start.1 = (f32[4,64,1024]{2,1,0:T(8,128)S(1)}, f32[4,64,1024]{2,1,0:T(8,128)}, u32[]{:S(2)}) copy-start(f32[4,64,1024]{2,1,0:T(8,128)} %volume_ref.5) | copy-start | bytes 3145732
  48.1 16.4 %collective-permute-start.4 = (f32[520,128]{1,0:T(8,128)S(1)}, f32[520,128]{1,0:T(8,128)}, u32[]{:S(2)}, u32[]{:S(2)}) collective-permute-start(f32[520,128]{1,0:T(8,128)S(1)} %gather.1.near_ref), channel_id=1, source_target_pairs={{0,64},{64,0},{128,192},{192,128},{256,320},{320,256},{384,448},{4... | collective-permute-start | bytes 798728 | tf_op jit(solution)/shard_map/ppermute | solution.py:79
  78.1 37.9 %collective-permute-start.5 = (f32[4,2,16,1024]{3,2,1,0:T(8,128)S(1)}, f32[4,2,16,1024]{3,2,1,0:T(8,128)S(1)}, u32[]{:S(2)}, u32[]{:S(2)}) collective-permute-start(f32[4,2,16,1024]{3,2,1,0:T(8,128)S(1)} %get-tuple-element.15), channel_id=1, source_target_pairs={{0,1},{1,2},{2,3},{3,4},{4,5},{5,6},{6,7},{7,8},{8,9},{9,10},{10,1... | collective-permute-start | bytes 1572872 | tf_op jit(solution)/shard_map/ppermute | solution.py:100
  109.9 10.5 %collective-permute-start.6 = (f32[4,2,16,1024]{3,2,1,0:T(8,128)S(1)}, f32[4,2,16,1024]{3,2,1,0:T(8,128)S(1)}, u32[]{:S(2)}, u32[]{:S(2)}) collective-permute-start(f32[4,2,16,1024]{3,2,1,0:T(8,128)S(1)} %get-tuple-element.14), channel_id=1, source_target_pairs={{1,0},{2,1},{3,2},{4,3},{5,4},{6,5},{7,6},{8,7},{9,8},{10,9},{11,1... | collective-permute-start | bytes 1572872 | tf_op jit(solution)/shard_map/ppermute | solution.py:105

commit v4 on v3

--- a/solution.py
+++ b/solution.py
@@ -161,7 +161,7 @@
     )(coefs, window, volume, measured)
 
 
-def spread_kernel(coef_ref, sums_ref, own_ref, next_ref, earlier_ref, out_ref):
+def spread_kernel(coef_ref, sums_ref, own_ref, next_ref, out_ref):
     count, layers = coef_ref.shape
     ring = out_ref.shape[0]
     columns = own_ref.shape[1]
@@ -190,20 +190,20 @@
     lax.fori_loop(0, ring, chunk, 0)
 
 
-def spread(coefs, sums, own, following, earlier, height, ring):
+def spread(coefs, sums, own, following, height, ring):
     layers, columns = coefs.shape[1], own.shape[1]
     length = layers * (height // ring) * columns // LANES + TILE
     return pl.pallas_call(
         spread_kernel,
-        in_specs=[SMEM, VMEM, VMEM, VMEM, ANY],
+        in_specs=[SMEM, VMEM, VMEM, VMEM],
         out_specs=VMEM,
         out_shape=jax.ShapeDtypeStruct((ring, length, LANES), jnp.float32),
         compiler_params=pltpu.CompilerParams(vmem_limit_bytes=8 * 2**20),
         name="spread",
-    )(coefs, sums, own, following, earlier)
-
-
-def gather_kernel(parts_ref, mine_ref):
+    )(coefs, sums, own, following)
+
+
+def gather_kernel(parts_ref, earlier_ref, mine_ref):
     ring, length, _ = parts_ref.shape
     step = next(n for n in (5 * TILE, 3 * TILE, TILE) if length % n == 0)
 
@@ -218,15 +218,15 @@
     lax.fori_loop(0, length // step, add, 0)
 
 
-def gather(parts):
+def gather(parts, earlier):
     return pl.pallas_call(
         gather_kernel,
-        in_specs=[VMEM],
+        in_specs=[VMEM, ANY],
         out_specs=VMEM,
         out_shape=jax.ShapeDtypeStruct(parts.shape[1:], jnp.float32),
         compiler_params=pltpu.CompilerParams(vmem_limit_bytes=8 * 2**20),
         name="gather",
-    )(parts)
+    )(parts, earlier)
 
 
 def late_kernel(volume_ref, window_ref, earlier_ref, whole_ref, window_out_ref):
@@ -489,8 +489,8 @@
     sums = jnp.concatenate([normal_before, normal_own, column_part[:, None]], axis=1)
     sums = jnp.pad(sums, ((0, TILE - layers), (0, LANES - 2 * layers - 1)))
 
-    sent = spread(back_coefs, sums, back, following, before, height, ring)
-    near = gather(over_ring(sent))
+    sent = spread(back_coefs, sums, back, following, height, ring)
+    near = gather(over_ring(sent), before)
     field = over_ring(update(place, near, from_far(near), before, volume, ring))
     residual, done = residual_of(flat(high_before), before, back, measured.shape)
     halo_low = to_next(field[:, layers - HALO :])

time: 126 us -> 125 us (level)
  the two profiles are of different devices: /device:TPU:89 before, /device:TPU:209 now
where the time goes in v4:
time: 125 us; the launch traced here: 124 us
  waiting for transfers between devices  53.6 us (43%)
  starting transfers between devices  33.9 us (27%)
  blocking collectives  16.7 us (13%)
  Pallas kernels  13.6 us (11%)
  local copies, waits for them, and re-layouts  2.81 us (2%)
  between operations  2.13 us (2%)
  other arithmetic  1.55 us (1%)
    ppermute x1, waiting for transfers between devices, from_far(): lax.ppermute(block, 'ang', [(a, a ^ 1) for a in range(lax.axis_size('ang'...  25.9 us
    all_to_all x1, blocking collectives, over_ring(): lax.all_to_all(pieces, 'ang', split_axis=0, concat_axis=0, axis_index_gro...  16.7 us
    all_to_all x1, waiting for transfers between devices, over_ring(): lax.all_to_all(pieces, 'ang', split_axis=0, concat_axis=0, axis_index_gro...  14.1 us
    ppermute x2, starting transfers between devices, to_next(): return lax.ppermute(block, ('ang', 'slab'), route(pairs))  11.8 us
    ppermute x2, waiting for transfers between devices, to_previous(): return lax.ppermute(block, ('ang', 'slab'), route(pairs))  11.2 us
    ppermute x1, starting transfers between devices, from_far(): lax.ppermute(block, 'ang', [(a, a ^ 1) for a in range(lax.axis_size('ang'...  9.27 us
    pallas_call x1, Pallas kernels, smooth(): pl.pallas_call(smooth_kernel, in_specs=[SMEM, ANY, VMEM, VMEM, VMEM], out...  4.95 us
    ppermute x2, starting transfers between devices, to_previous(): return lax.ppermute(block, ('ang', 'slab'), route(pairs))  4.5 us
  transfers between devices with their start and end apart: 8, of which 5 were waited for; matrix products, arithmetic and copies ran while one was open for 1% of the time, Pallas kernels for 4%

profile of v4, /device:TPU:209, one launch (start us, length us, event | category | flops | bytes accessed | tf_op | source)
XLA Modules:
  0.0 124.3 jit_solution(16374740536419679824)
XLA Ops:
  2.0 0.8 multiply_reduce_fusion
  2.8 0.1 reshape.147
  2.9 1.2 copy-done
  4.1 1.0 copy-done.2
  5.1 0.9 pack.1.earlier_ref.own_ref
  6.0 2.6 %collective-permute-start.3 = (f32[264,1024]{1,0:T(8,128)S(1)}, f32[264,1024]{1,0:T(8,128)S(1)}, u32[]{:S(2)}, u32[]{:S(2)}) collective-permute-start(f32[264,1024]{1,0:T(8,128)S(1)} %pack.1.earlier_ref.own_ref), channel_id=1, source_target_pairs={{1,0},{2,1},{3,2},{4,3},{5,4},{6,5},{7,6},{8,7},{9,8},{10,9},{11,1... | collective-permute-start | bytes 3244040 | tf_op jit(solution)/shard_map/ppermute | solution.py:105
  8.6 3.4 %collective-permute-start = (f32[2,4,4]{2,1,0:T(4,128)S(1)}, f32[2,4,4]{2,1,0:T(4,128)S(1)}, u32[]{:S(2)}, u32[]{:S(2)}) collective-permute-start(f32[2,4,4]{2,1,0:T(4,128)S(1)} %get-tuple-element.11.window_ref), channel_id=1, source_target_pairs={{0,1},{1,2},{2,3},{3,4},{4,5},{5,6},{6,7},{7,8},{8,9},{9,10},{10,1... | collective-permute-start | bytes 392 | tf_op jit(solution)/shard_map/ppermute | solution.py:16
  12.1 1.0 late.1
  13.1 0.6 collective-permute-start.2
  13.8 2.4 %collective-permute-start.1 = (f32[4,64,1024]{2,1,0:T(8,128)}, f32[4,64,1024]{2,1,0:T(8,128)S(1)}, u32[]{:S(2)}, u32[]{:S(2)}) collective-permute-start(f32[4,64,1024]{2,1,0:T(8,128)} %get-tuple-element.6), channel_id=1, source_target_pairs={{0,1},{1,2},{2,3},{3,4},{4,5},{5,6},{6,7},{7,8},{8,9},{9,10},{10,1... | collective-permute-start | bytes 3145736 | tf_op jit(solution)/shard_map/ppermute | solution.py:100
  16.2 0.1 copy.8
  16.3 0.1 slice_reduce_fusion.3
  16.4 0.1 fusion.2
  16.5 6.8 %collective-permute-done.3.next_ref = f32[264,1024]{1,0:T(8,128)S(1)} collective-permute-done((f32[264,1024]{1,0:T(8,128)S(1)}, f32[264,1024]{1,0:T(8,128)S(1)}, u32[]{:S(2)}, u32[]{:S(2)}) %collective-permute-start.3) | collective-permute-done | bytes 1081376 | tf_op jit(solution)/shard_map/ppermute | solution.py:105
  23.3 0.1 reshape_squeeze.3
  23.4 0.1 slice_reduce_fusion
  23.5 0.1 div.30
  23.8 0.1 multiply_reduce_fusion.2
  24.1 2.2 %spread.1 = f32[4,520,128]{2,1,0:T(8,128)} custom-call(f32[8,4]{1,0:T(8,128)S(1)} %pad_maximum_fusion.coef_ref, f32[8,128]{1,0:T(8,128)S(1)} %select_maximum_fusion.sums_ref, f32[264,1024]{1,0:T(8,128)S(1)} %pack.1.earlier_ref.own_ref, f32[264,1024]{1,0:T(8,128)S(1)} %collective-permute-done.3.next_ref), custom_call_target="tpu_custom_call" | custom-call | tf_op jit(solution)/shard_map/spread/pallas_call | solution.py:196
  26.3 4.2 %all-to-all-start = ((f32[4,520,128]{2,1,0:T(8,128)}), f32[4,520,128]{2,1,0:T(8,128)}, u32[]{:S(2)}, u32[]{:S(2)}) async-start(f32[4,520,128]{2,1,0:T(8,128)} %spread.1), calls=%async_computation | async-start | bytes 2129920 | tf_op jit(solution)/shard_map/all_to_all | solution.py:60
  30.5 14.1 %all-to-all-done.parts_ref = f32[4,520,128]{2,1,0:T(8,128)} async-done(((f32[4,520,128]{2,1,0:T(8,128)}), f32[4,520,128]{2,1,0:T(8,128)}, u32[]{:S(2)}, u32[]{:S(2)}) %all-to-all-start) | async-done | bytes 1064992 | tf_op jit(solution)/shard_map/all_to_all | solution.py:60
  44.7 1.3 %gather.1.near_ref = f32[520,128]{1,0:T(8,128)S(1)} custom-call(f32[4,520,128]{2,1,0:T(8,128)} %all-to-all-done.parts_ref, f32[4,64,1024]{2,1,0:T(8,128)S(1)} %collective-permute-done.1.before_ref.earlier_ref), custom_call_target="tpu_custom_call" | custom-call | tf_op jit(solution)/shard_map/gather/pallas_call | solution.py:222
  46.0 9.3 %collective-permute-start.4 = (f32[520,128]{1,0:T(8,128)S(1)}, f32[520,128]{1,0:T(8,128)}, u32[]{:S(2)}, u32[]{:S(2)}) collective-permute-start(f32[520,128]{1,0:T(8,128)S(1)} %gather.1.near_ref), channel_id=1, source_target_pairs={{0,64},{64,0},{128,192},{192,128},{256,320},{320,256},{384,448},{4... | collective-permute-start | bytes 798728 | tf_op jit(solution)/shard_map/ppermute | solution.py:79
  55.4 25.9 %collective-permute-done.4.far_ref = f32[520,128]{1,0:T(8,128)} collective-permute-done((f32[520,128]{1,0:T(8,128)S(1)}, f32[520,128]{1,0:T(8,128)}, u32[]{:S(2)}, u32[]{:S(2)}) %collective-permute-start.4) | collective-permute-done | bytes 266272 | tf_op jit(solution)/shard_map/ppermute | solution.py:79
  81.3 1.3 %update.1 = f32[4,4,16,1024]{3,2,1,0:T(8,128)S(1)} custom-call(s32[3]{0:T(128)S(1)} %pad_add_fusion.place_ref, f32[520,128]{1,0:T(8,128)S(1)} %gather.1.near_ref, f32[520,128]{1,0:T(8,128)} %collective-permute-done.4.far_ref, f32[4,64,1024]{2,1,0:T(8,128)S(1)} %collective-permute-done.1.before_ref.earlier_ref, f32[4,64,1024]{2,1,0:T(8,128)S(1)} %copy-done.1), custom_call_target="tpu_custom_call" | custom-call | tf_op jit(solution)/shard_map/update/pallas_call | solution.py:326
  82.6 16.7 %all_to_all.10.own_ref = f32[4,4,16,1024]{3,2,1,0:T(8,128)S(1)} all-to-all(f32[4,4,16,1024]{3,2,1,0:T(8,128)S(1)} %update.1), channel_id=1, replica_groups={{0,128,256,384},{64,192,320,448},{1,129,257,385},{65,193,321,449},{2,13..., dimensions={0} | all-to-all | bytes 2097152 | tf_op jit(solution)/shard_map/all_to_all | solution.py:60
  99.4 9.4 %collective-permute-start.5 = (f32[4,2,16,1024]{3,2,1,0:T(8,128)S(1)}, f32[4,2,16,1024]{3,2,1,0:T(8,128)S(1)}, u32[]{:S(2)}, u32[]{:S(2)}) collective-permute-start(f32[4,2,16,1024]{3,2,1,0:T(8,128)S(1)} %get-tuple-element.15), channel_id=1, source_target_pairs={{0,1},{1,2},{2,3},{3,4},{4,5},{5,6},{6,7},{7,8},{8,9},{9,10},{10,1... | collective-permute-start | bytes 1572872 | tf_op jit(solution)/shard_map/ppermute | solution.py:100
  108.8 1.9 %collective-permute-start.6 = (f32[4,2,16,1024]{3,2,1,0:T(8,128)S(1)}, f32[4,2,16,1024]{3,2,1,0:T(8,128)S(1)}, u32[]{:S(2)}, u32[]{:S(2)}) collective-permute-start(f32[4,2,16,1024]{3,2,1,0:T(8,128)S(1)} %get-tuple-element.14), channel_id=1, source_target_pairs={{1,0},{2,1},{3,2},{4,3},{5,4},{6,5},{7,6},{8,7},{9,8},{10,9},{11,1... | collective-permute-start | bytes 1572872 | tf_op jit(solution)/shard_map/ppermute | solution.py:105
  110.8 1.8 %residual.1 = (f32[2,2,64,1024]{3,2,1,0:T(8,128)}, f32[8,128]{1,0:T(8,128)S(1)}) custom-call(f32[4,4]{1,0:T(4,128)S(1)} %bitcast.12, f32[4,64,1024]{2,1,0:T(8,128)S(1)} %collective-permute-done.1.before_ref.earlier_ref, f32[264,1024]{1,0:T(8,128)S(1)} %pack.1.earlier_ref.own_ref), custom_call_target="tpu_custom_call" | custom-call | bytes 16777216 | tf_op jit(solution)/shard_map/residual/pallas_call | solution.py:281
  112.6 2.3 %collective-permute-done.5.low_ref = f32[4,2,16,1024]{3,2,1,0:T(8,128)S(1)} collective-permute-done((f32[4,2,16,1024]{3,2,1,0:T(8,128)S(1)}, f32[4,2,16,1024]{3,2,1,0:T(8,128)S(1)}, u32[]{:S(2)}, u32[]{:S(2)}) %collective-permute-start.5) | collective-permute-done | bytes 524320 | tf_op jit(solution)/shard_map/ppermute | solution.py:100
  114.9 4.4 %collective-permute-done.6.high_ref = f32[4,2,16,1024]{3,2,1,0:T(8,128)S(1)} collective-permute-done((f32[4,2,16,1024]{3,2,1,0:T(8,128)S(1)}, f32[4,2,16,1024]{3,2,1,0:T(8,128)S(1)}, u32[]{:S(2)}, u32[]{:S(2)}) %collective-permute-start.6) | collective-permute-done | bytes 524320 | tf_op jit(solution)/shard_map/ppermute | solution.py:105
  119.3 5.0 %smooth.1 = f32[4,64,1024]{2,1,0:T(8,128)} custom-call(s32[3]{0:T(128)S(1)} %pad_add_fusion.place_ref, f32[8,128]{1,0:T(8,128)S(1)} %get-tuple-element.7.earlier_ref, f32[4,4,16,1024]{3,2,1,0:T(8,128)S(1)} %all_to_all.10.own_ref, f32[4,2,16,1024]{3,2,1,0:T(8,128)S(1)} %collective-permute-done.5.low_ref, f32[4,2,16,1024]{3,2,1,0:T(8,128)S(1)} %collective-permute-done.6.high_ref), custom_call_target="tpu_custom_call" | custom-call | tf_op jit(solution)/shard_map/smooth/pallas_call | solution.py:430
  (22 shorter events, 0.6 us)
Async XLA Ops:
  2.8 1.2 copy-start
  4.1 1.0 copy-start.2
  6.0 17.3 %collective-permute-start.3 = (f32[264,1024]{1,0:T(8,128)S(1)}, f32[264,1024]{1,0:T(8,128)S(1)}, u32[]{:S(2)}, u32[]{:S(2)}) collective-permute-start(f32[264,1024]{1,0:T(8,128)S(1)} %pack.1.earlier_ref.own_ref), channel_id=1, source_target_pairs={{1,0},{2,1},{3,2},{4,3},{5,4},{6,5},{7,6},{8,7},{9,8},{10,9},{11,1... | collective-permute-start | bytes 3244040 | tf_op jit(solution)/shard_map/ppermute | solution.py:105
  8.6 7.7 %collective-permute-start = (f32[2,4,4]{2,1,0:T(4,128)S(1)}, f32[2,4,4]{2,1,0:T(4,128)S(1)}, u32[]{:S(2)}, u32[]{:S(2)}) collective-permute-start(f32[2,4,4]{2,1,0:T(4,128)S(1)} %get-tuple-element.11.window_ref), channel_id=1, source_target_pairs={{0,1},{1,2},{2,3},{3,4},{4,5},{5,6},{6,7},{7,8},{8,9},{9,10},{10,1... | collective-permute-start | bytes 392 | tf_op jit(solution)/shard_map/ppermute | solution.py:16
  13.1 3.3 %collective-permute-start.2 = (f32[2,4,4]{2,1,0:T(4,128)S(1)}, f32[2,4,4]{2,1,0:T(4,128)S(1)}, u32[]{:S(2)}, u32[]{:S(2)}) collective-permute-start(f32[2,4,4]{2,1,0:T(4,128)S(1)} %get-tuple-element.8), channel_id=1, source_target_pairs={{15,79},{31,95},{47,111},{63,127},{79,15},{95,31},{111,47},{127,63... | collective-permute-start | bytes 392 | tf_op jit(solution)/shard_map/ppermute | solution.py:95
  13.8 16.8 %collective-permute-start.1 = (f32[4,64,1024]{2,1,0:T(8,128)}, f32[4,64,1024]{2,1,0:T(8,128)S(1)}, u32[]{:S(2)}, u32[]{:S(2)}) collective-permute-start(f32[4,64,1024]{2,1,0:T(8,128)} %get-tuple-element.6), channel_id=1, source_target_pairs={{0,1},{1,2},{2,3},{3,4},{4,5},{5,6},{6,7},{7,8},{8,9},{9,10},{10,1... | collective-permute-start | bytes 3145736 | tf_op jit(solution)/shard_map/ppermute | solution.py:100
  26.3 18.4 %all-to-all-start = ((f32[4,520,128]{2,1,0:T(8,128)}), f32[4,520,128]{2,1,0:T(8,128)}, u32[]{:S(2)}, u32[]{:S(2)}) async-start(f32[4,520,128]{2,1,0:T(8,128)} %spread.1), calls=%async_computation | async-start | bytes 2129920 | tf_op jit(solution)/shard_map/all_to_all | solution.py:60
  30.5 50.8 %copy-start.1 = (f32[4,64,1024]{2,1,0:T(8,128)S(1)}, f32[4,64,1024]{2,1,0:T(8,128)}, u32[]{:S(2)}) copy-start(f32[4,64,1024]{2,1,0:T(8,128)} %volume_ref.5) | copy-start | bytes 3145732
  46.0 35.3 %collective-permute-start.4 = (f32[520,128]{1,0:T(8,128)S(1)}, f32[520,128]{1,0:T(8,128)}, u32[]{:S(2)}, u32[]{:S(2)}) collective-permute-start(f32[520,128]{1,0:T(8,128)S(1)} %gather.1.near_ref), channel_id=1, source_target_pairs={{0,64},{64,0},{128,192},{192,128},{256,320},{320,256},{384,448},{4... | collective-permute-start | bytes 798728 | tf_op jit(solution)/shard_map/ppermute | solution.py:79
  99.4 15.5 %collective-permute-start.5 = (f32[4,2,16,1024]{3,2,1,0:T(8,128)S(1)}, f32[4,2,16,1024]{3,2,1,0:T(8,128)S(1)}, u32[]{:S(2)}, u32[]{:S(2)}) collective-permute-start(f32[4,2,16,1024]{3,2,1,0:T(8,128)S(1)} %get-tuple-element.15), channel_id=1, source_target_pairs={{0,1},{1,2},{2,3},{3,4},{4,5},{5,6},{6,7},{7,8},{8,9},{9,10},{10,1... | collective-permute-start | bytes 1572872 | tf_op jit(solution)/shard_map/ppermute | solution.py:100
  108.8 10.5 %collective-permute-start.6 = (f32[4,2,16,1024]{3,2,1,0:T(8,128)S(1)}, f32[4,2,16,1024]{3,2,1,0:T(8,128)S(1)}, u32[]{:S(2)}, u32[]{:S(2)}) collective-permute-start(f32[4,2,16,1024]{3,2,1,0:T(8,128)S(1)} %get-tuple-element.14), channel_id=1, source_target_pairs={{1,0},{2,1},{3,2},{4,3},{5,4},{6,5},{7,6},{8,7},{9,8},{10,9},{11,1... | collective-permute-start | bytes 1572872 | tf_op jit(solution)/shard_map/ppermute | solution.py:105

commit v5 on v4

--- a/solution.py
+++ b/solution.py
@@ -40,8 +40,23 @@
     ]
 
 
+def along_column(block, distance):
+    count, slabs = lax.axis_size("ang"), lax.axis_size("slab")
+    pairs = []
+    for a in range(count):
+        for t in range(slabs):
+            there = ((a % 2 * ROW + t % ROW) // 2 + distance) % ROW
+            to_ang = a - a % 2 + there * 2 // ROW
+            to_slab = t - t % ROW + there * 2 % ROW + t % 2
+            pairs.append((a * slabs + t, to_ang * slabs + to_slab))
+    return lax.ppermute(block, ("ang", "slab"), pairs)
+
+
 def from_far(block):
-    return lax.ppermute(block, "ang", [(a, a ^ 1) for a in range(lax.axis_size("ang"))])
+    half = (block.shape[0] // TILE + 1) // 2 * TILE
+    most = ROW // 2 - 1
+    up, down = along_column(block[:half], most), along_column(block[half:], -most)
+    return jnp.concatenate([along_column(up, 1), along_column(down, -1)])
 
 
 def from_far_at_row_ends(block):

time: 125 us -> 125 us (level)
  no operation moved by 1% of the time
where the time goes in v5:
time: 125 us; the launch traced here: 124 us
  waiting for transfers between devices  53.6 us (43%)
  starting transfers between devices  33.9 us (27%)
  blocking collectives  16.7 us (13%)
  Pallas kernels  13.6 us (11%)
  local copies, waits for them, and re-layouts  2.81 us (2%)
  between operations  2.13 us (2%)
  other arithmetic  1.55 us (1%)
    ppermute x1, waiting for transfers between devices, from_far(): lax.ppermute(block, 'ang', [(a, a ^ 1) for a in range(lax.axis_size('ang'...  25.9 us
    all_to_all x1, blocking collectives, over_ring(): lax.all_to_all(pieces, 'ang', split_axis=0, concat_axis=0, axis_index_gro...  16.7 us
    all_to_all x1, waiting for transfers between devices, over_ring(): lax.all_to_all(pieces, 'ang', split_axis=0, concat_axis=0, axis_index_gro...  14.1 us
    ppermute x2, starting transfers between devices, to_next(): return lax.ppermute(block, ('ang', 'slab'), route(pairs))  11.8 us
    ppermute x2, waiting for transfers between devices, to_previous(): return lax.ppermute(block, ('ang', 'slab'), route(pairs))  11.2 us
    ppermute x1, starting transfers between devices, from_far(): lax.ppermute(block, 'ang', [(a, a ^ 1) for a in range(lax.axis_size('ang'...  9.27 us
    pallas_call x1, Pallas kernels, smooth(): pl.pallas_call(smooth_kernel, in_specs=[SMEM, ANY, VMEM, VMEM, VMEM], out...  4.95 us
    ppermute x2, starting transfers between devices, to_previous(): return lax.ppermute(block, ('ang', 'slab'), route(pairs))  4.5 us
  transfers between devices with their start and end apart: 8, of which 5 were waited for; matrix products, arithmetic and copies ran while one was open for 1% of the time, Pallas kernels for 4%

profile of v5, /device:TPU:209, one launch (start us, length us, event | category | flops | bytes accessed | tf_op | source)
XLA Modules:
  0.0 124.3 jit_solution(16374740536419679824)
XLA Ops:
  2.0 0.8 multiply_reduce_fusion
  2.8 0.1 reshape.147
  2.9 1.2 copy-done
  4.1 1.0 copy-done.2
  5.1 0.9 pack.1.earlier_ref.own_ref
  6.0 2.6 %collective-permute-start.3 = (f32[264,1024]{1,0:T(8,128)S(1)}, f32[264,1024]{1,0:T(8,128)S(1)}, u32[]{:S(2)}, u32[]{:S(2)}) collective-permute-start(f32[264,1024]{1,0:T(8,128)S(1)} %pack.1.earlier_ref.own_ref), channel_id=1, source_target_pairs={{1,0},{2,1},{3,2},{4,3},{5,4},{6,5},{7,6},{8,7},{9,8},{10,9},{11,1... | collective-permute-start | bytes 3244040 | tf_op jit(solution)/shard_map/ppermute | solution.py:120
  8.6 3.4 %collective-permute-start = (f32[2,4,4]{2,1,0:T(4,128)S(1)}, f32[2,4,4]{2,1,0:T(4,128)S(1)}, u32[]{:S(2)}, u32[]{:S(2)}) collective-permute-start(f32[2,4,4]{2,1,0:T(4,128)S(1)} %get-tuple-element.11.window_ref), channel_id=1, source_target_pairs={{0,1},{1,2},{2,3},{3,4},{4,5},{5,6},{6,7},{7,8},{8,9},{9,10},{10,1... | collective-permute-start | bytes 392 | tf_op jit(solution)/shard_map/ppermute | solution.py:16
  12.1 1.0 late.1
  13.1 0.6 collective-permute-start.2
  13.8 2.4 %collective-permute-start.1 = (f32[4,64,1024]{2,1,0:T(8,128)}, f32[4,64,1024]{2,1,0:T(8,128)S(1)}, u32[]{:S(2)}, u32[]{:S(2)}) collective-permute-start(f32[4,64,1024]{2,1,0:T(8,128)} %get-tuple-element.6), channel_id=1, source_target_pairs={{0,1},{1,2},{2,3},{3,4},{4,5},{5,6},{6,7},{7,8},{8,9},{9,10},{10,1... | collective-permute-start | bytes 3145736 | tf_op jit(solution)/shard_map/ppermute | solution.py:115
  16.2 0.1 copy.8
  16.3 0.1 slice_reduce_fusion.3
  16.4 0.1 fusion.2
  16.5 6.8 %collective-permute-done.3.next_ref = f32[264,1024]{1,0:T(8,128)S(1)} collective-permute-done((f32[264,1024]{1,0:T(8,128)S(1)}, f32[264,1024]{1,0:T(8,128)S(1)}, u32[]{:S(2)}, u32[]{:S(2)}) %collective-permute-start.3) | collective-permute-done | bytes 1081376 | tf_op jit(solution)/shard_map/ppermute | solution.py:120
  23.3 0.1 reshape_squeeze.3
  23.4 0.1 slice_reduce_fusion
  23.5 0.1 div.30
  23.8 0.1 multiply_reduce_fusion.2
  24.1 2.2 %spread.1 = f32[4,520,128]{2,1,0:T(8,128)} custom-call(f32[8,4]{1,0:T(8,128)S(1)} %pad_maximum_fusion.coef_ref, f32[8,128]{1,0:T(8,128)S(1)} %select_maximum_fusion.sums_ref, f32[264,1024]{1,0:T(8,128)S(1)} %pack.1.earlier_ref.own_ref, f32[264,1024]{1,0:T(8,128)S(1)} %collective-permute-done.3.next_ref), custom_call_target="tpu_custom_call" | custom-call | tf_op jit(solution)/shard_map/spread/pallas_call | solution.py:211
  26.3 4.2 %all-to-all-start = ((f32[4,520,128]{2,1,0:T(8,128)}), f32[4,520,128]{2,1,0:T(8,128)}, u32[]{:S(2)}, u32[]{:S(2)}) async-start(f32[4,520,128]{2,1,0:T(8,128)} %spread.1), calls=%async_computation | async-start | bytes 2129920 | tf_op jit(solution)/shard_map/all_to_all | solution.py:75
  30.5 14.1 %all-to-all-done.parts_ref = f32[4,520,128]{2,1,0:T(8,128)} async-done(((f32[4,520,128]{2,1,0:T(8,128)}), f32[4,520,128]{2,1,0:T(8,128)}, u32[]{:S(2)}, u32[]{:S(2)}) %all-to-all-start) | async-done | bytes 1064992 | tf_op jit(solution)/shard_map/all_to_all | solution.py:75
  44.7 1.3 %gather.1.near_ref = f32[520,128]{1,0:T(8,128)S(1)} custom-call(f32[4,520,128]{2,1,0:T(8,128)} %all-to-all-done.parts_ref, f32[4,64,1024]{2,1,0:T(8,128)S(1)} %collective-permute-done.1.before_ref.earlier_ref), custom_call_target="tpu_custom_call" | custom-call | tf_op jit(solution)/shard_map/gather/pallas_call | solution.py:237
  46.0 9.3 %collective-permute-start.4 = (f32[520,128]{1,0:T(8,128)S(1)}, f32[520,128]{1,0:T(8,128)}, u32[]{:S(2)}, u32[]{:S(2)}) collective-permute-start(f32[520,128]{1,0:T(8,128)S(1)} %gather.1.near_ref), channel_id=1, source_target_pairs={{0,64},{64,0},{128,192},{192,128},{256,320},{320,256},{384,448},{4... | collective-permute-start | bytes 798728 | tf_op jit(solution)/shard_map/ppermute | solution.py:94
  55.4 25.9 %collective-permute-done.4.far_ref = f32[520,128]{1,0:T(8,128)} collective-permute-done((f32[520,128]{1,0:T(8,128)S(1)}, f32[520,128]{1,0:T(8,128)}, u32[]{:S(2)}, u32[]{:S(2)}) %collective-permute-start.4) | collective-permute-done | bytes 266272 | tf_op jit(solution)/shard_map/ppermute | solution.py:94
  81.3 1.3 %update.1 = f32[4,4,16,1024]{3,2,1,0:T(8,128)S(1)} custom-call(s32[3]{0:T(128)S(1)} %pad_add_fusion.place_ref, f32[520,128]{1,0:T(8,128)S(1)} %gather.1.near_ref, f32[520,128]{1,0:T(8,128)} %collective-permute-done.4.far_ref, f32[4,64,1024]{2,1,0:T(8,128)S(1)} %collective-permute-done.1.before_ref.earlier_ref, f32[4,64,1024]{2,1,0:T(8,128)S(1)} %copy-done.1), custom_call_target="tpu_custom_call" | custom-call | tf_op jit(solution)/shard_map/update/pallas_call | solution.py:341
  82.6 16.7 %all_to_all.10.own_ref = f32[4,4,16,1024]{3,2,1,0:T(8,128)S(1)} all-to-all(f32[4,4,16,1024]{3,2,1,0:T(8,128)S(1)} %update.1), channel_id=1, replica_groups={{0,128,256,384},{64,192,320,448},{1,129,257,385},{65,193,321,449},{2,13..., dimensions={0} | all-to-all | bytes 2097152 | tf_op jit(solution)/shard_map/all_to_all | solution.py:75
  99.4 9.4 %collective-permute-start.5 = (f32[4,2,16,1024]{3,2,1,0:T(8,128)S(1)}, f32[4,2,16,1024]{3,2,1,0:T(8,128)S(1)}, u32[]{:S(2)}, u32[]{:S(2)}) collective-permute-start(f32[4,2,16,1024]{3,2,1,0:T(8,128)S(1)} %get-tuple-element.15), channel_id=1, source_target_pairs={{0,1},{1,2},{2,3},{3,4},{4,5},{5,6},{6,7},{7,8},{8,9},{9,10},{10,1... | collective-permute-start | bytes 1572872 | tf_op jit(solution)/shard_map/ppermute | solution.py:115
  108.8 1.9 %collective-permute-start.6 = (f32[4,2,16,1024]{3,2,1,0:T(8,128)S(1)}, f32[4,2,16,1024]{3,2,1,0:T(8,128)S(1)}, u32[]{:S(2)}, u32[]{:S(2)}) collective-permute-start(f32[4,2,16,1024]{3,2,1,0:T(8,128)S(1)} %get-tuple-element.14), channel_id=1, source_target_pairs={{1,0},{2,1},{3,2},{4,3},{5,4},{6,5},{7,6},{8,7},{9,8},{10,9},{11,1... | collective-permute-start | bytes 1572872 | tf_op jit(solution)/shard_map/ppermute | solution.py:120
  110.8 1.8 %residual.1 = (f32[2,2,64,1024]{3,2,1,0:T(8,128)}, f32[8,128]{1,0:T(8,128)S(1)}) custom-call(f32[4,4]{1,0:T(4,128)S(1)} %bitcast.12, f32[4,64,1024]{2,1,0:T(8,128)S(1)} %collective-permute-done.1.before_ref.earlier_ref, f32[264,1024]{1,0:T(8,128)S(1)} %pack.1.earlier_ref.own_ref), custom_call_target="tpu_custom_call" | custom-call | bytes 16777216 | tf_op jit(solution)/shard_map/residual/pallas_call | solution.py:296
  112.6 2.3 %collective-permute-done.5.low_ref = f32[4,2,16,1024]{3,2,1,0:T(8,128)S(1)} collective-permute-done((f32[4,2,16,1024]{3,2,1,0:T(8,128)S(1)}, f32[4,2,16,1024]{3,2,1,0:T(8,128)S(1)}, u32[]{:S(2)}, u32[]{:S(2)}) %collective-permute-start.5) | collective-permute-done | bytes 524320 | tf_op jit(solution)/shard_map/ppermute | solution.py:115
  114.9 4.4 %collective-permute-done.6.high_ref = f32[4,2,16,1024]{3,2,1,0:T(8,128)S(1)} collective-permute-done((f32[4,2,16,1024]{3,2,1,0:T(8,128)S(1)}, f32[4,2,16,1024]{3,2,1,0:T(8,128)S(1)}, u32[]{:S(2)}, u32[]{:S(2)}) %collective-permute-start.6) | collective-permute-done | bytes 524320 | tf_op jit(solution)/shard_map/ppermute | solution.py:120
  119.3 5.0 %smooth.1 = f32[4,64,1024]{2,1,0:T(8,128)} custom-call(s32[3]{0:T(128)S(1)} %pad_add_fusion.place_ref, f32[8,128]{1,0:T(8,128)S(1)} %get-tuple-element.7.earlier_ref, f32[4,4,16,1024]{3,2,1,0:T(8,128)S(1)} %all_to_all.10.own_ref, f32[4,2,16,1024]{3,2,1,0:T(8,128)S(1)} %collective-permute-done.5.low_ref, f32[4,2,16,1024]{3,2,1,0:T(8,128)S(1)} %collective-permute-done.6.high_ref), custom_call_target="tpu_custom_call" | custom-call | tf_op jit(solution)/shard_map/smooth/pallas_call | solution.py:445
  (22 shorter events, 0.6 us)
Async XLA Ops:
  2.8 1.2 copy-start
  4.1 1.0 copy-start.2
  6.0 17.3 %collective-permute-start.3 = (f32[264,1024]{1,0:T(8,128)S(1)}, f32[264,1024]{1,0:T(8,128)S(1)}, u32[]{:S(2)}, u32[]{:S(2)}) collective-permute-start(f32[264,1024]{1,0:T(8,128)S(1)} %pack.1.earlier_ref.own_ref), channel_id=1, source_target_pairs={{1,0},{2,1},{3,2},{4,3},{5,4},{6,5},{7,6},{8,7},{9,8},{10,9},{11,1... | collective-permute-start | bytes 3244040 | tf_op jit(solution)/shard_map/ppermute | solution.py:120
  8.6 7.7 %collective-permute-start = (f32[2,4,4]{2,1,0:T(4,128)S(1)}, f32[2,4,4]{2,1,0:T(4,128)S(1)}, u32[]{:S(2)}, u32[]{:S(2)}) collective-permute-start(f32[2,4,4]{2,1,0:T(4,128)S(1)} %get-tuple-element.11.window_ref), channel_id=1, source_target_pairs={{0,1},{1,2},{2,3},{3,4},{4,5},{5,6},{6,7},{7,8},{8,9},{9,10},{10,1... | collective-permute-start | bytes 392 | tf_op jit(solution)/shard_map/ppermute | solution.py:16
  13.1 3.3 %collective-permute-start.2 = (f32[2,4,4]{2,1,0:T(4,128)S(1)}, f32[2,4,4]{2,1,0:T(4,128)S(1)}, u32[]{:S(2)}, u32[]{:S(2)}) collective-permute-start(f32[2,4,4]{2,1,0:T(4,128)S(1)} %get-tuple-element.8), channel_id=1, source_target_pairs={{15,79},{31,95},{47,111},{63,127},{79,15},{95,31},{111,47},{127,63... | collective-permute-start | bytes 392 | tf_op jit(solution)/shard_map/ppermute | solution.py:110
  13.8 16.8 %collective-permute-start.1 = (f32[4,64,1024]{2,1,0:T(8,128)}, f32[4,64,1024]{2,1,0:T(8,128)S(1)}, u32[]{:S(2)}, u32[]{:S(2)}) collective-permute-start(f32[4,64,1024]{2,1,0:T(8,128)} %get-tuple-element.6), channel_id=1, source_target_pairs={{0,1},{1,2},{2,3},{3,4},{4,5},{5,6},{6,7},{7,8},{8,9},{9,10},{10,1... | collective-permute-start | bytes 3145736 | tf_op jit(solution)/shard_map/ppermute | solution.py:115
  26.3 18.4 %all-to-all-start = ((f32[4,520,128]{2,1,0:T(8,128)}), f32[4,520,128]{2,1,0:T(8,128)}, u32[]{:S(2)}, u32[]{:S(2)}) async-start(f32[4,520,128]{2,1,0:T(8,128)} %spread.1), calls=%async_computation | async-start | bytes 2129920 | tf_op jit(solution)/shard_map/all_to_all | solution.py:75
  30.5 50.8 %copy-start.1 = (f32[4,64,1024]{2,1,0:T(8,128)S(1)}, f32[4,64,1024]{2,1,0:T(8,128)}, u32[]{:S(2)}) copy-start(f32[4,64,1024]{2,1,0:T(8,128)} %volume_ref.5) | copy-start | bytes 3145732
  46.0 35.3 %collective-permute-start.4 = (f32[520,128]{1,0:T(8,128)S(1)}, f32[520,128]{1,0:T(8,128)}, u32[]{:S(2)}, u32[]{:S(2)}) collective-permute-start(f32[520,128]{1,0:T(8,128)S(1)} %gather.1.near_ref), channel_id=1, source_target_pairs={{0,64},{64,0},{128,192},{192,128},{256,320},{320,256},{384,448},{4... | collective-permute-start | bytes 798728 | tf_op jit(solution)/shard_map/ppermute | solution.py:94
  99.4 15.5 %collective-permute-start.5 = (f32[4,2,16,1024]{3,2,1,0:T(8,128)S(1)}, f32[4,2,16,1024]{3,2,1,0:T(8,128)S(1)}, u32[]{:S(2)}, u32[]{:S(2)}) collective-permute-start(f32[4,2,16,1024]{3,2,1,0:T(8,128)S(1)} %get-tuple-element.15), channel_id=1, source_target_pairs={{0,1},{1,2},{2,3},{3,4},{4,5},{5,6},{6,7},{7,8},{8,9},{9,10},{10,1... | collective-permute-start | bytes 1572872 | tf_op jit(solution)/shard_map/ppermute | solution.py:115
  108.8 10.5 %collective-permute-start.6 = (f32[4,2,16,1024]{3,2,1,0:T(8,128)S(1)}, f32[4,2,16,1024]{3,2,1,0:T(8,128)S(1)}, u32[]{:S(2)}, u32[]{:S(2)}) collective-permute-start(f32[4,2,16,1024]{3,2,1,0:T(8,128)S(1)} %get-tuple-element.14), channel_id=1, source_target_pairs={{1,0},{2,1},{3,2},{4,3},{5,4},{6,5},{7,6},{8,7},{9,8},{10,9},{11,1... | collective-permute-start | bytes 1572872 | tf_op jit(solution)/shard_map/ppermute | solution.py:120

commit v6 on v5

--- a/solution.py
+++ b/solution.py
@@ -55,8 +55,8 @@
 def from_far(block):
     half = (block.shape[0] // TILE + 1) // 2 * TILE
     most = ROW // 2 - 1
-    up, down = along_column(block[:half], most), along_column(block[half:], -most)
-    return jnp.concatenate([along_column(up, 1), along_column(down, -1)])
+    up, down = along_column(block[:half], 1), along_column(block[half:], -1)
+    return jnp.concatenate([along_column(up, most), along_column(down, -most)])
 
 
 def from_far_at_row_ends(block):

time: 125 us -> 125 us (level)
  no operation moved by 1% of the time
where the time goes in v6:
time: 125 us; the launch traced here: 124 us
  waiting for transfers between devices  53.6 us (43%)
  starting transfers between devices  33.9 us (27%)
  blocking collectives  16.7 us (13%)
  Pallas kernels  13.6 us (11%)
  local copies, waits for them, and re-layouts  2.81 us (2%)
  between operations  2.13 us (2%)
  other arithmetic  1.55 us (1%)
    ppermute x1, waiting for transfers between devices, from_far(): lax.ppermute(block, 'ang', [(a, a ^ 1) for a in range(lax.axis_size('ang'...  25.9 us
    all_to_all x1, blocking collectives, over_ring(): lax.all_to_all(pieces, 'ang', split_axis=0, concat_axis=0, axis_index_gro...  16.7 us
    all_to_all x1, waiting for transfers between devices, over_ring(): lax.all_to_all(pieces, 'ang', split_axis=0, concat_axis=0, axis_index_gro...  14.1 us
    ppermute x2, starting transfers between devices, to_next(): return lax.ppermute(block, ('ang', 'slab'), route(pairs))  11.8 us
    ppermute x2, waiting for transfers between devices, to_previous(): return lax.ppermute(block, ('ang', 'slab'), route(pairs))  11.2 us
    ppermute x1, starting transfers between devices, from_far(): lax.ppermute(block, 'ang', [(a, a ^ 1) for a in range(lax.axis_size('ang'...  9.27 us
    pallas_call x1, Pallas kernels, smooth(): pl.pallas_call(smooth_kernel, in_specs=[SMEM, ANY, VMEM, VMEM, VMEM], out...  4.95 us
    ppermute x2, starting transfers between devices, to_previous(): return lax.ppermute(block, ('ang', 'slab'), route(pairs))  4.5 us
  transfers between devices with their start and end apart: 8, of which 5 were waited for; matrix products, arithmetic and copies ran while one was open for 1% of the time, Pallas kernels for 4%

profile of v6, /device:TPU:209, one launch (start us, length us, event | category | flops | bytes accessed | tf_op | source)
XLA Modules:
  0.0 124.3 jit_solution(16374740536419679824)
XLA Ops:
  2.0 0.8 multiply_reduce_fusion
  2.8 0.1 reshape.147
  2.9 1.2 copy-done
  4.1 1.0 copy-done.2
  5.1 0.9 pack.1.earlier_ref.own_ref
  6.0 2.6 %collective-permute-start.3 = (f32[264,1024]{1,0:T(8,128)S(1)}, f32[264,1024]{1,0:T(8,128)S(1)}, u32[]{:S(2)}, u32[]{:S(2)}) collective-permute-start(f32[264,1024]{1,0:T(8,128)S(1)} %pack.1.earlier_ref.own_ref), channel_id=1, source_target_pairs={{1,0},{2,1},{3,2},{4,3},{5,4},{6,5},{7,6},{8,7},{9,8},{10,9},{11,1... | collective-permute-start | bytes 3244040 | tf_op jit(solution)/shard_map/ppermute | solution.py:120
  8.6 3.4 %collective-permute-start = (f32[2,4,4]{2,1,0:T(4,128)S(1)}, f32[2,4,4]{2,1,0:T(4,128)S(1)}, u32[]{:S(2)}, u32[]{:S(2)}) collective-permute-start(f32[2,4,4]{2,1,0:T(4,128)S(1)} %get-tuple-element.11.window_ref), channel_id=1, source_target_pairs={{0,1},{1,2},{2,3},{3,4},{4,5},{5,6},{6,7},{7,8},{8,9},{9,10},{10,1... | collective-permute-start | bytes 392 | tf_op jit(solution)/shard_map/ppermute | solution.py:16
  12.1 1.0 late.1
  13.1 0.6 collective-permute-start.2
  13.8 2.4 %collective-permute-start.1 = (f32[4,64,1024]{2,1,0:T(8,128)}, f32[4,64,1024]{2,1,0:T(8,128)S(1)}, u32[]{:S(2)}, u32[]{:S(2)}) collective-permute-start(f32[4,64,1024]{2,1,0:T(8,128)} %get-tuple-element.6), channel_id=1, source_target_pairs={{0,1},{1,2},{2,3},{3,4},{4,5},{5,6},{6,7},{7,8},{8,9},{9,10},{10,1... | collective-permute-start | bytes 3145736 | tf_op jit(solution)/shard_map/ppermute | solution.py:115
  16.2 0.1 copy.8
  16.3 0.1 slice_reduce_fusion.3
  16.4 0.1 fusion.2
  16.5 6.8 %collective-permute-done.3.next_ref = f32[264,1024]{1,0:T(8,128)S(1)} collective-permute-done((f32[264,1024]{1,0:T(8,128)S(1)}, f32[264,1024]{1,0:T(8,128)S(1)}, u32[]{:S(2)}, u32[]{:S(2)}) %collective-permute-start.3) | collective-permute-done | bytes 1081376 | tf_op jit(solution)/shard_map/ppermute | solution.py:120
  23.3 0.1 reshape_squeeze.3
  23.4 0.1 slice_reduce_fusion
  23.5 0.1 div.30
  23.8 0.1 multiply_reduce_fusion.2
  24.1 2.2 %spread.1 = f32[4,520,128]{2,1,0:T(8,128)} custom-call(f32[8,4]{1,0:T(8,128)S(1)} %pad_maximum_fusion.coef_ref, f32[8,128]{1,0:T(8,128)S(1)} %select_maximum_fusion.sums_ref, f32[264,1024]{1,0:T(8,128)S(1)} %pack.1.earlier_ref.own_ref, f32[264,1024]{1,0:T(8,128)S(1)} %collective-permute-done.3.next_ref), custom_call_target="tpu_custom_call" | custom-call | tf_op jit(solution)/shard_map/spread/pallas_call | solution.py:211
  26.3 4.2 %all-to-all-start = ((f32[4,520,128]{2,1,0:T(8,128)}), f32[4,520,128]{2,1,0:T(8,128)}, u32[]{:S(2)}, u32[]{:S(2)}) async-start(f32[4,520,128]{2,1,0:T(8,128)} %spread.1), calls=%async_computation | async-start | bytes 2129920 | tf_op jit(solution)/shard_map/all_to_all | solution.py:75
  30.5 14.1 %all-to-all-done.parts_ref = f32[4,520,128]{2,1,0:T(8,128)} async-done(((f32[4,520,128]{2,1,0:T(8,128)}), f32[4,520,128]{2,1,0:T(8,128)}, u32[]{:S(2)}, u32[]{:S(2)}) %all-to-all-start) | async-done | bytes 1064992 | tf_op jit(solution)/shard_map/all_to_all | solution.py:75
  44.7 1.3 %gather.1.near_ref = f32[520,128]{1,0:T(8,128)S(1)} custom-call(f32[4,520,128]{2,1,0:T(8,128)} %all-to-all-done.parts_ref, f32[4,64,1024]{2,1,0:T(8,128)S(1)} %collective-permute-done.1.before_ref.earlier_ref), custom_call_target="tpu_custom_call" | custom-call | tf_op jit(solution)/shard_map/gather/pallas_call | solution.py:237
  46.0 9.3 %collective-permute-start.4 = (f32[520,128]{1,0:T(8,128)S(1)}, f32[520,128]{1,0:T(8,128)}, u32[]{:S(2)}, u32[]{:S(2)}) collective-permute-start(f32[520,128]{1,0:T(8,128)S(1)} %gather.1.near_ref), channel_id=1, source_target_pairs={{0,64},{64,0},{128,192},{192,128},{256,320},{320,256},{384,448},{4... | collective-permute-start | bytes 798728 | tf_op jit(solution)/shard_map/ppermute | solution.py:94
  55.4 25.9 %collective-permute-done.4.far_ref = f32[520,128]{1,0:T(8,128)} collective-permute-done((f32[520,128]{1,0:T(8,128)S(1)}, f32[520,128]{1,0:T(8,128)}, u32[]{:S(2)}, u32[]{:S(2)}) %collective-permute-start.4) | collective-permute-done | bytes 266272 | tf_op jit(solution)/shard_map/ppermute | solution.py:94
  81.3 1.3 %update.1 = f32[4,4,16,1024]{3,2,1,0:T(8,128)S(1)} custom-call(s32[3]{0:T(128)S(1)} %pad_add_fusion.place_ref, f32[520,128]{1,0:T(8,128)S(1)} %gather.1.near_ref, f32[520,128]{1,0:T(8,128)} %collective-permute-done.4.far_ref, f32[4,64,1024]{2,1,0:T(8,128)S(1)} %collective-permute-done.1.before_ref.earlier_ref, f32[4,64,1024]{2,1,0:T(8,128)S(1)} %copy-done.1), custom_call_target="tpu_custom_call" | custom-call | tf_op jit(solution)/shard_map/update/pallas_call | solution.py:341
  82.6 16.7 %all_to_all.10.own_ref = f32[4,4,16,1024]{3,2,1,0:T(8,128)S(1)} all-to-all(f32[4,4,16,1024]{3,2,1,0:T(8,128)S(1)} %update.1), channel_id=1, replica_groups={{0,128,256,384},{64,192,320,448},{1,129,257,385},{65,193,321,449},{2,13..., dimensions={0} | all-to-all | bytes 2097152 | tf_op jit(solution)/shard_map/all_to_all | solution.py:75
  99.4 9.4 %collective-permute-start.5 = (f32[4,2,16,1024]{3,2,1,0:T(8,128)S(1)}, f32[4,2,16,1024]{3,2,1,0:T(8,128)S(1)}, u32[]{:S(2)}, u32[]{:S(2)}) collective-permute-start(f32[4,2,16,1024]{3,2,1,0:T(8,128)S(1)} %get-tuple-element.15), channel_id=1, source_target_pairs={{0,1},{1,2},{2,3},{3,4},{4,5},{5,6},{6,7},{7,8},{8,9},{9,10},{10,1... | collective-permute-start | bytes 1572872 | tf_op jit(solution)/shard_map/ppermute | solution.py:115
  108.8 1.9 %collective-permute-start.6 = (f32[4,2,16,1024]{3,2,1,0:T(8,128)S(1)}, f32[4,2,16,1024]{3,2,1,0:T(8,128)S(1)}, u32[]{:S(2)}, u32[]{:S(2)}) collective-permute-start(f32[4,2,16,1024]{3,2,1,0:T(8,128)S(1)} %get-tuple-element.14), channel_id=1, source_target_pairs={{1,0},{2,1},{3,2},{4,3},{5,4},{6,5},{7,6},{8,7},{9,8},{10,9},{11,1... | collective-permute-start | bytes 1572872 | tf_op jit(solution)/shard_map/ppermute | solution.py:120
  110.8 1.8 %residual.1 = (f32[2,2,64,1024]{3,2,1,0:T(8,128)}, f32[8,128]{1,0:T(8,128)S(1)}) custom-call(f32[4,4]{1,0:T(4,128)S(1)} %bitcast.12, f32[4,64,1024]{2,1,0:T(8,128)S(1)} %collective-permute-done.1.before_ref.earlier_ref, f32[264,1024]{1,0:T(8,128)S(1)} %pack.1.earlier_ref.own_ref), custom_call_target="tpu_custom_call" | custom-call | bytes 16777216 | tf_op jit(solution)/shard_map/residual/pallas_call | solution.py:296
  112.6 2.3 %collective-permute-done.5.low_ref = f32[4,2,16,1024]{3,2,1,0:T(8,128)S(1)} collective-permute-done((f32[4,2,16,1024]{3,2,1,0:T(8,128)S(1)}, f32[4,2,16,1024]{3,2,1,0:T(8,128)S(1)}, u32[]{:S(2)}, u32[]{:S(2)}) %collective-permute-start.5) | collective-permute-done | bytes 524320 | tf_op jit(solution)/shard_map/ppermute | solution.py:115
  114.9 4.4 %collective-permute-done.6.high_ref = f32[4,2,16,1024]{3,2,1,0:T(8,128)S(1)} collective-permute-done((f32[4,2,16,1024]{3,2,1,0:T(8,128)S(1)}, f32[4,2,16,1024]{3,2,1,0:T(8,128)S(1)}, u32[]{:S(2)}, u32[]{:S(2)}) %collective-permute-start.6) | collective-permute-done | bytes 524320 | tf_op jit(solution)/shard_map/ppermute | solution.py:120
  119.3 5.0 %smooth.1 = f32[4,64,1024]{2,1,0:T(8,128)} custom-call(s32[3]{0:T(128)S(1)} %pad_add_fusion.place_ref, f32[8,128]{1,0:T(8,128)S(1)} %get-tuple-element.7.earlier_ref, f32[4,4,16,1024]{3,2,1,0:T(8,128)S(1)} %all_to_all.10.own_ref, f32[4,2,16,1024]{3,2,1,0:T(8,128)S(1)} %collective-permute-done.5.low_ref, f32[4,2,16,1024]{3,2,1,0:T(8,128)S(1)} %collective-permute-done.6.high_ref), custom_call_target="tpu_custom_call" | custom-call | tf_op jit(solution)/shard_map/smooth/pallas_call | solution.py:445
  (22 shorter events, 0.6 us)
Async XLA Ops:
  2.8 1.2 copy-start
  4.1 1.0 copy-start.2
  6.0 17.3 %collective-permute-start.3 = (f32[264,1024]{1,0:T(8,128)S(1)}, f32[264,1024]{1,0:T(8,128)S(1)}, u32[]{:S(2)}, u32[]{:S(2)}) collective-permute-start(f32[264,1024]{1,0:T(8,128)S(1)} %pack.1.earlier_ref.own_ref), channel_id=1, source_target_pairs={{1,0},{2,1},{3,2},{4,3},{5,4},{6,5},{7,6},{8,7},{9,8},{10,9},{11,1... | collective-permute-start | bytes 3244040 | tf_op jit(solution)/shard_map/ppermute | solution.py:120
  8.6 7.7 %collective-permute-start = (f32[2,4,4]{2,1,0:T(4,128)S(1)}, f32[2,4,4]{2,1,0:T(4,128)S(1)}, u32[]{:S(2)}, u32[]{:S(2)}) collective-permute-start(f32[2,4,4]{2,1,0:T(4,128)S(1)} %get-tuple-element.11.window_ref), channel_id=1, source_target_pairs={{0,1},{1,2},{2,3},{3,4},{4,5},{5,6},{6,7},{7,8},{8,9},{9,10},{10,1... | collective-permute-start | bytes 392 | tf_op jit(solution)/shard_map/ppermute | solution.py:16
  13.1 3.3 %collective-permute-start.2 = (f32[2,4,4]{2,1,0:T(4,128)S(1)}, f32[2,4,4]{2,1,0:T(4,128)S(1)}, u32[]{:S(2)}, u32[]{:S(2)}) collective-permute-start(f32[2,4,4]{2,1,0:T(4,128)S(1)} %get-tuple-element.8), channel_id=1, source_target_pairs={{15,79},{31,95},{47,111},{63,127},{79,15},{95,31},{111,47},{127,63... | collective-permute-start | bytes 392 | tf_op jit(solution)/shard_map/ppermute | solution.py:110
  13.8 16.8 %collective-permute-start.1 = (f32[4,64,1024]{2,1,0:T(8,128)}, f32[4,64,1024]{2,1,0:T(8,128)S(1)}, u32[]{:S(2)}, u32[]{:S(2)}) collective-permute-start(f32[4,64,1024]{2,1,0:T(8,128)} %get-tuple-element.6), channel_id=1, source_target_pairs={{0,1},{1,2},{2,3},{3,4},{4,5},{5,6},{6,7},{7,8},{8,9},{9,10},{10,1... | collective-permute-start | bytes 3145736 | tf_op jit(solution)/shard_map/ppermute | solution.py:115
  26.3 18.4 %all-to-all-start = ((f32[4,520,128]{2,1,0:T(8,128)}), f32[4,520,128]{2,1,0:T(8,128)}, u32[]{:S(2)}, u32[]{:S(2)}) async-start(f32[4,520,128]{2,1,0:T(8,128)} %spread.1), calls=%async_computation | async-start | bytes 2129920 | tf_op jit(solution)/shard_map/all_to_all | solution.py:75
  30.5 50.8 %copy-start.1 = (f32[4,64,1024]{2,1,0:T(8,128)S(1)}, f32[4,64,1024]{2,1,0:T(8,128)}, u32[]{:S(2)}) copy-start(f32[4,64,1024]{2,1,0:T(8,128)} %volume_ref.5) | copy-start | bytes 3145732
  46.0 35.3 %collective-permute-start.4 = (f32[520,128]{1,0:T(8,128)S(1)}, f32[520,128]{1,0:T(8,128)}, u32[]{:S(2)}, u32[]{:S(2)}) collective-permute-start(f32[520,128]{1,0:T(8,128)S(1)} %gather.1.near_ref), channel_id=1, source_target_pairs={{0,64},{64,0},{128,192},{192,128},{256,320},{320,256},{384,448},{4... | collective-permute-start | bytes 798728 | tf_op jit(solution)/shard_map/ppermute | solution.py:94
  99.4 15.5 %collective-permute-start.5 = (f32[4,2,16,1024]{3,2,1,0:T(8,128)S(1)}, f32[4,2,16,1024]{3,2,1,0:T(8,128)S(1)}, u32[]{:S(2)}, u32[]{:S(2)}) collective-permute-start(f32[4,2,16,1024]{3,2,1,0:T(8,128)S(1)} %get-tuple-element.15), channel_id=1, source_target_pairs={{0,1},{1,2},{2,3},{3,4},{4,5},{5,6},{6,7},{7,8},{8,9},{9,10},{10,1... | collective-permute-start | bytes 1572872 | tf_op jit(solution)/shard_map/ppermute | solution.py:115
  108.8 10.5 %collective-permute-start.6 = (f32[4,2,16,1024]{3,2,1,0:T(8,128)S(1)}, f32[4,2,16,1024]{3,2,1,0:T(8,128)S(1)}, u32[]{:S(2)}, u32[]{:S(2)}) collective-permute-start(f32[4,2,16,1024]{3,2,1,0:T(8,128)S(1)} %get-tuple-element.14), channel_id=1, source_target_pairs={{1,0},{2,1},{3,2},{4,3},{5,4},{6,5},{7,6},{8,7},{9,8},{10,9},{11,1... | collective-permute-start | bytes 1572872 | tf_op jit(solution)/shard_map/ppermute | solution.py:120
